TPU v7x, 32 devices: a whole 2x2x4 slice. The times are simulated.
32 devices in a mesh: replica: 2 (over y), shard: 8 (over z, x), ctx: 2 (over core).
Axes of the slice: x: 2, y: 2, z: 4, core: 2. Of those that a mesh axis runs over, the one named last changes fastest.
Arguments:
- layer_input: bfloat16 [64, 512, 1024], P(('replica', 'shard'), 'ctx'), may hold values from -6 to 6
- segment_ids: int32 [64, 512], P(('replica', 'shard')), may hold values from 0 to 4, as said below
- out_cotangent: bfloat16 [64, 512, 1024], P(('replica', 'shard'), 'ctx'), may hold values from -6 to 6
- attn_master: float32 [4, 1024, 1024], P(None, 'shard')
- inner_master: float32 [1024, 4096], P('shard'), may hold values from -0.1875 to 0.1875
- outer_master: float32 [4096, 1024], P('shard'), may hold values from -0.09375 to 0.09375
- vector_master: float32 [12, 1024], P(None, 'shard')
- attn_moment: float32 [4, 1024, 1024], P(None, 'shard')
- inner_moment: float32 [1024, 4096], P('shard')
- outer_moment: float32 [4096, 1024], P('shard')
- vector_moment: float32 [12, 1024], P(None, 'shard')
- attn_square: float32 [4, 1024, 1024], P(None, 'shard'), as said below
- inner_square: float32 [1024, 4096], P('shard'), as said below
- outer_square: float32 [4096, 1024], P('shard'), as said below
- vector_square: float32 [12, 1024], P(None, 'shard'), as said below
Outputs:
- layer_output: bfloat16 [64, 512, 1024], P(('replica', 'shard'), 'ctx')
- input_grad: float32 [64, 512, 1024], P(('replica', 'shard'), 'ctx')
- attn_moment_new: float32 [4, 1024, 1024], P(None, 'shard')
- inner_moment_new: float32 [1024, 4096], P('shard')
- outer_moment_new: float32 [4096, 1024], P('shard')
- vector_moment_new: float32 [12, 1024], P(None, 'shard')
- attn_square_new: float32 [4, 1024, 1024], P(None, 'shard')
- inner_square_new: float32 [1024, 4096], P('shard')
- outer_square_new: float32 [4096, 1024], P('shard')
- vector_square_new: float32 [12, 1024], P(None, 'shard')
- attn_new: float32 [4, 1024, 1024], P(None, 'shard')
- inner_new: float32 [1024, 4096], P('shard')
- outer_new: float32 [4096, 1024], P('shard')
- vector_new: float32 [12, 1024], P(None, 'shard')
- attn_low: bfloat16 [4, 1024, 1024], P(None, 'shard')
- inner_low: bfloat16 [1024, 4096], P('shard')
- outer_low: bfloat16 [4096, 1024], P('shard')
- vector_low: bfloat16 [12, 1024], P(None, 'shard')
Inputs may be any that keep to these rules, and one draw needn't show every extreme that they name: `segment_ids`: along each sequence the ids never fall, start at 0 and end at 4; positions 192 to 320 carry one id. `attn_square`: every entry is positive. `inner_square`: every entry is positive. `outer_square`: every entry is positive. `vector_square`: every entry is positive.
All inputs are finite; a program needn't handle non-finite values.
Results may differ from a plain program's by a relative error of at most 0.024.
Values may be sent and summed in bfloat16 or wider, within the bound.
No kernel may reach another device: no remote copies, remote signals or barrier semaphores. Data moves between devices by JAX's collectives and lax.ppermute only.
A program may use at most 320 MiB of HBM per device.

v0:
```python
import functools
import math

import jax
import jax.numpy as jnp
from jax import lax
from jax.experimental import pallas as pl
from jax.experimental.pallas import tpu as pltpu
from jax.sharding import PartitionSpec as P

HD = 64
PAIR = 2 * HD
STEP = 5
OUTER = 4
EVERY = ("shard", "replica", "ctx")

EPS_NORM = 1e-05
BETA_ONE = 0.5
BETA_TWO = 0.6
RATE_MATRIX = 0.02
RATE_VECTOR = 0.1
DECAY = 0.01
EPS_ADAM = 1e-06
MASKED = -1e30
F32 = jnp.float32
BF16 = jnp.bfloat16
PARTS = 32
TILE = 32
VMEM = 56 * 1024 * 1024
SMALL_VMEM = 16 * 1024 * 1024
GROUP = 256
NT = (((1,), (1,)), ((), ()))
TN = (((0,), (0,)), ((), ()))


def weight_of(micros):
    return pl.CostEstimate(
        flops=int(micros * 2.9e8), bytes_accessed=int(micros * 9.2e5), transcendentals=0
    )


def normalize(resid):
    centre = resid - jnp.mean(resid, -1, keepdims=True)
    scale = lax.rsqrt(jnp.mean(centre * centre, -1, keepdims=True) + EPS_NORM)
    return (centre * scale, scale)


def norm_back(grad, normed, scale):
    return scale * (
        grad
        - jnp.mean(grad, -1, keepdims=True)
        - normed * jnp.mean(grad * normed, -1, keepdims=True)
    )


def adamw(grad, moment, square, weight, rate):
    moment_new = BETA_ONE * moment + (1.0 - BETA_ONE) * grad
    square_new = BETA_TWO * square + (1.0 - BETA_TWO) * grad * grad
    stepped = (
        moment_new
        / (1.0 - BETA_ONE**STEP)
        / (jnp.sqrt(square_new / (1.0 - BETA_TWO**STEP)) + EPS_ADAM)
    )
    weight_new = weight - rate * (stepped + DECAY * weight)
    return (moment_new, square_new, weight_new)


def swap_cores(value):
    return lax.ppermute(value, "ctx", [(0, 1), (1, 0)])


def shift_outer(value, step):
    inner = lax.axis_size("shard") // OUTER
    pairs = [
        (o * inner + i, ((o + step) % OUTER) * inner + i) for o in range(OUTER) for i in range(inner)
    ]
    return lax.ppermute(value, "shard", pairs)


def shift_inner(value, step):
    inner = lax.axis_size("shard") // OUTER
    pairs = [
        (o * inner + i, o * inner + (i + step) % inner) for o in range(OUTER) for i in range(inner)
    ]
    return lax.ppermute(value, "shard", pairs)


def shift_replica(value, step):
    size = lax.axis_size("replica")
    return lax.ppermute(value, "replica", [(r, (r + step) % size) for r in range(size)])


def ring_gather(piece):
    inner = lax.axis_size("shard") // OUTER
    found = []
    held = piece
    for k in range(OUTER):
        if k:
            held = shift_outer(held, -1)
        found.append([held] + [shift_inner(held, -e) for e in range(1, inner)])
    return [item for group in found for item in group]


def slot_owners():
    inner = lax.axis_size("shard") // OUTER
    at = lax.axis_index("shard")
    o, i = at // inner, at % inner
    return [
        lax.rem(o + k, OUTER) * inner + lax.rem(i + e, inner)
        for k in range(OUTER)
        for e in range(inner)
    ]


def pick(array, index, axis):
    return lax.dynamic_index_in_dim(array, index, axis, keepdims=False)


def add_low(value, *others):
    total = value.astype(F32)
    for item in others:
        total = total + item.astype(F32)
    return total.astype(BF16)


def position():
    inner = lax.axis_size("shard") // OUTER
    at = lax.axis_index("shard")
    return at // inner, at % inner, lax.axis_index("replica"), inner


def is_square():
    return lax.axis_size("replica") == 2 and lax.axis_size("shard") == 2 * OUTER


def swap_outer(value, flip):
    inner = lax.axis_size("shard") // OUTER
    pairs = [(o * inner + i, (o ^ flip) * inner + i) for o in range(OUTER) for i in range(inner)]
    return lax.ppermute(value, "shard", pairs)


def swap_cross(value):
    return lax.ppermute(value, ("replica", "ctx"), [(a, 3 - a) for a in range(4)])


def sum_apart(chip_sum):
    o, i, y, inner = position()
    grid = chip_sum.reshape(OUTER, inner, *chip_sum.shape[1:])
    got = [shift_inner(pick(grid, lax.rem(i + e, inner), 1), e) for e in range(1, inner)]
    line = add_low(pick(grid, i, 1), *got)
    got = [shift_outer(pick(line, lax.rem(o + d, OUTER), 0), d) for d in range(1, OUTER)]
    total = add_low(pick(line, o, 0), *got)
    got = [shift_replica(total, r) for r in range(1, lax.axis_size("replica"))]
    mine = add_low(total, *got)[None]
    return [mine, swap_cores(mine)]


def small_call(kernel, where, ins, outs, after, name):
    held = pl.BlockSpec(memory_space=pltpu.VMEM)
    return pl.pallas_call(
        functools.partial(kernel, len(ins), len(after)),
        in_specs=[pl.BlockSpec(memory_space=pltpu.SMEM)]
        + [held] * len(ins)
        + [pl.BlockSpec(memory_space=pl.ANY)] * len(after),
        out_specs=[held] * len(outs),
        out_shape=[pltpu.VMEM(shape, BF16) for shape in outs],
        compiler_params=pltpu.CompilerParams(vmem_limit_bytes=SMALL_VMEM),
        cost_estimate=weight_of(1),
        name=name,
    )(where, *[pltpu.with_memory_space_constraint(a, pltpu.VMEM) for a in ins], *after)


def fold_plane_kernel(count, after, where_ref, keep_p, got_p, keep_q, got_q, *rest):
    i, y = where_ref[1], where_ref[2]
    kept_p, send_p, kept_q, send_q = rest[after:]
    for o in range(OUTER):
        for out, at in ((kept_p, y), (send_p, 1 - y)):
            out[o] = add_low(keep_p[o, at], got_p[o, at])
        for out, at in ((kept_q, i), (send_q, 1 - i)):
            out[o] = add_low(keep_q[o, at], got_q[o, at])


def line_order(o):
    near = o + 1 - 2 * lax.rem(o, 2)
    far = lambda at: lax.rem(at + 2, OUTER)
    return (o, far(o)), (near, far(near))


def fold_cross_kernel(count, after, where_ref, keep_p, got_p, keep_q, got_q, *rest):
    for out, order in zip(rest[after:], line_order(where_ref[0])):
        for n, at in enumerate(order):
            out[n, 0] = add_low(keep_p[at], got_p[at])
            out[n, 1] = add_low(keep_q[at], got_q[at])


def fold_turn_kernel(count, after, where_ref, keep, got, *rest):
    for n, out in enumerate(rest[after:]):
        out[...] = add_low(keep[n], got[n])


def fold_line_kernel(count, after, where_ref, *rest):
    rest[count + after][...] = add_low(*(ref[...] for ref in rest[:count]))


def merge_kernel(groups, after, where_ref, *refs):
    outs = refs[4 * sum(groups) + after :]
    for slot, out in enumerate(outs):
        left = chip = 0
        for group in groups:
            for at in range(2):
                parts = []
                for n in range(chip, chip + group):
                    ref = refs[4 * n + slot]
                    parts.append(ref[0, at, 0, 0] if slot % 2 else ref[0, 0, 0, at])
                cut = slice(left, left + parts[0].shape[1])
                out[0, at, :, cut] = parts[0] if group == 1 else add_low(*parts)
            left, chip = cut.stop, chip + group


class Sum:
    def __init__(self, where, *groups):
        self.where, self.rows = where, groups[0][0].shape[1] // 4
        self.columns = sum(group[0].shape[2] for group in groups)
        self.groups = [len(group) for group in groups]
        self.chips = [
            c.reshape(OUTER, 2, 2, 2, self.rows, c.shape[2]) for group in groups for c in group
        ]

    def shape(self, *lead):
        return lead + (self.rows, self.columns)

    def merge(self, after=()):
        def spec(chip, lead, flip):
            def place(o, w):
                at = w[1] if lead == 0 else w[2]
                at = 1 - at if flip else at
                return (o, at, 0, 0, 0, 0) if lead == 0 else (o, 0, 1, at, 0, 0)

            return pl.BlockSpec(((1, 1, 1, 2) if lead == 0 else (1, 2, 1, 1)) + chip.shape[4:], place)

        kinds = ((0, True), (1, True), (0, False), (1, False))
        out_spec = pl.BlockSpec((1, 2, self.rows, self.columns), lambda o, w: (o, 0, 0, 0))
        *sent, keep_p, keep_q = pl.pallas_call(
            functools.partial(merge_kernel, self.groups, len(after)),
            grid_spec=pltpu.PrefetchScalarGridSpec(
                num_scalar_prefetch=1,
                grid=(OUTER,),
                in_specs=[spec(chip, *kind) for chip in self.chips for kind in kinds]
                + [pl.BlockSpec(memory_space=pl.ANY)] * len(after),
                out_specs=[out_spec] * 4,
            ),
            out_shape=[jax.ShapeDtypeStruct(self.shape(OUTER, 2), BF16)] * 4,
            compiler_params=pltpu.CompilerParams(vmem_limit_bytes=SMALL_VMEM),
            cost_estimate=weight_of(4),
            name="merge",
        )(self.where, *[chip for chip in self.chips for _ in range(4)], *after)
        self.kept = [keep_p, shift_inner(sent[0], 1), keep_q, shift_replica(sent[1], 1)]
        return tuple(sent)

    def plane(self, after=()):
        keep_p, send_p, keep_q, send_q = small_call(
            fold_plane_kernel, self.where, self.kept, [self.shape(OUTER)] * 4, after, "fold_plane"
        )
        self.kept = [keep_p, shift_replica(send_p, 1), keep_q, shift_inner(send_q, 1)]
        return (send_p, send_q)

    def cross(self, after=()):
        keep, send = small_call(
            fold_cross_kernel, self.where, self.kept, [self.shape(2, 2)] * 2, after, "fold_cross"
        )
        self.kept = [keep, swap_outer(send, 1)]
        return (send,)

    def turn(self, after=()):
        shapes = [self.kept[0].shape[1:]] * 2
        keep, send = small_call(
            fold_turn_kernel, self.where, self.kept, shapes, after, "fold_turn"
        )
        self.kept = [keep, swap_outer(send, 2)]
        return (send,)

    def line(self, after=()):
        (total,) = small_call(
            fold_line_kernel, self.where, self.kept, [self.kept[0].shape], after, "fold_line"
        )
        self.shares = [total, shift_replica(total, 1), swap_cores(total), swap_cross(total)]
        return (total,)


def update_kernel(groups, after, where_ref, *refs):
    states, shares = refs[:3], refs[3 : 3 + sum(groups)]
    outs, grad_ref = refs[3 + sum(groups) + after : -1], refs[-1]
    rows = shares[0].shape[1]
    across = groups[0] // 2
    for core in range(2):

        @pl.when(pl.program_id(1) == core)
        def _():
            for n in range(across):
                line = where_ref[2] if n == 0 else 1 - where_ref[2]
                line = pl.ds(pl.multiple_of(line * rows, rows), rows) if across > 1 else slice(None)
                if len(groups) == 1:
                    grad_ref[line, :] = shares[across * core + n][0].astype(F32)
                    continue
                left, right = shares[across * core + n], shares[groups[0] + across * core + n]
                width = grad_ref.shape[2]
                pairs = width // PAIR
                for t in range(3):
                    for p in range(pairs):
                        side, at = (left, p) if 2 * p < pairs else (right, p - pairs // 2)
                        part = side[0, :, (3 * at + t) * PAIR : (3 * at + t + 1) * PAIR]
                        grad_ref[t, line, p * PAIR : (p + 1) * PAIR] = part.astype(F32)
                cut = 3 * PAIR * (pairs // 2)
                grad_ref[3, line, :] = left[0, :, cut : cut + width].astype(F32)

    new = adamw(grad_ref[...], states[1][...], states[2][...], states[0][...], RATE_MATRIX)
    for out, value in zip(outs, new + (new[2],)):
        out[...] = value.astype(out.dtype)


def update(where, states, groups, after=()):
    parts, rows = groups[0][0].shape[:2]
    rows = rows * (len(groups[0]) // 2)
    lead = states[0].shape[:-2]
    columns = states[0].shape[-1] // 2
    place = lambda p, v, w: (0,) * len(lead) + (p, w[3] + v - 2 * w[3] * v)
    block = pl.BlockSpec(lead + (rows, columns), place)
    shares = [share for group in groups for share in group]
    share_specs = [pl.BlockSpec((1,) + a.shape[1:], lambda p, v, w: (p, 0, 0)) for a in shares]
    kinds = (F32, F32, F32, BF16)
    return pl.pallas_call(
        functools.partial(update_kernel, [len(group) for group in groups], len(after)),
        grid_spec=pltpu.PrefetchScalarGridSpec(
            num_scalar_prefetch=1,
            grid=(parts, 2),
            in_specs=[block] * 3 + share_specs + [pl.BlockSpec(memory_space=pl.ANY)] * len(after),
            out_specs=[block] * 4,
            scratch_shapes=[pltpu.VMEM(lead + (rows, columns), F32)],
        ),
        out_shape=[jax.ShapeDtypeStruct(states[0].shape, kind) for kind in kinds],
        compiler_params=pltpu.CompilerParams(vmem_limit_bytes=SMALL_VMEM),
        cost_estimate=weight_of(5),
        name="update",
    )(where, *states, *shares, *after)


def input_back_kernel(a_ref, b_ref, left_ref, right_ref, *rest):
    out_ref = rest[-1]
    total = lax.dot_general(a_ref[...], left_ref[...], NT, preferred_element_type=F32)
    total += lax.dot_general(b_ref[...], right_ref[...], NT, preferred_element_type=F32)
    if out_ref.dtype == F32:
        total += rest[0][...].astype(F32) + rest[1][...].astype(F32)
    out_ref[...] = total.astype(out_ref.dtype)


def input_back(grad_a, grad_b, weight, added, after):
    count, cut = grad_a.shape[0] // 2, grad_a.shape[1]
    width = weight.shape[0]
    tile = width // 4
    first = 0 if added else 1
    side = pl.BlockSpec((count, cut), lambda n: (first, 0))
    line = pl.BlockSpec((count, tile), lambda n: (0, n))
    return pl.pallas_call(
        input_back_kernel,
        grid=(width // tile,),
        in_specs=[side, side]
        + [pl.BlockSpec((tile, cut), lambda n, at=at: (n, at)) for at in range(2)]
        + [line] * len(added)
        + [pl.BlockSpec(memory_space=pl.ANY)] * len(after),
        out_specs=line,
        out_shape=jax.ShapeDtypeStruct((count, width), F32 if added else BF16),
        compiler_params=pltpu.CompilerParams(vmem_limit_bytes=SMALL_VMEM),
        cost_estimate=weight_of(5),
        name="input_back",
    )(*[grad_a, grad_b, weight, weight, *added], *after)


def quarter_places(order):
    o, i, y, inner = position()
    kinds = ((i, y), (1 - i, y), (i, 1 - y), (1 - i, 1 - y))
    return [(row * 2 + across, side) for across, side in kinds for row in order]


def relay_kernel(count, after, where_ref, *rest):
    for source, out in zip(rest[:count], rest[count + after :]):
        out[...] = source[...]


def halves_kernel(count, after, where_ref, near_x, near_y, *rest):
    first, second = rest[after:]
    first[...] = near_y[: OUTER // 2]
    second[...] = near_x[OUTER // 2 :]


def pair_kernel(count, after, where_ref, own, other, *rest):
    rest[after][0] = own[...]
    rest[after][1] = other[...]


def bulk_kernel(count, after, where_ref, *rest):
    ins, (bulk, *far) = rest[:count], rest[count + after :]
    at = 0
    for source in ins:
        bulk[at : at + source.shape[0]] = source[...]
        at += source.shape[0]
    for out, source in zip(far, (4, 3)):
        out[...] = ins[source][...]


def relay(where, arrays, after):
    return small_call(relay_kernel, where, arrays, [a.shape for a in arrays], after, "relay")


def project_kernel(after, row_ref, column_ref, mine_ref, theirs_ref, bias_ref, factor_ref, *rest):
    stacks, (out_ref, weight_ref) = rest[: -2 - after], rest[-2:]
    columns = stacks[0].shape[2]
    part = weight_ref.shape[0] * weight_ref.shape[1] // columns
    part = part // sum(stack.shape[0] for stack in stacks)
    at = pl.program_id(0)

    @pl.when(at == 0)
    def _():
        slot = 0
        for stack in stacks:
            for k in range(stack.shape[0]):
                start = pl.multiple_of(row_ref[slot] * part, part)
                left = pl.multiple_of(column_ref[slot] * columns, PAIR)
                weight_ref[pl.ds(start, part), pl.ds(left, columns)] = stack[k, :part, :]
                slot += 1

    def fill(rows):
        acc = jnp.dot(rows, weight_ref[...], preferred_element_type=F32)
        out_ref[...] = ((acc + bias_ref[...]) * factor_ref[...]).astype(BF16)

    @pl.when(at < pl.num_programs(0) // 2)
    def _():
        fill(mine_ref[...])

    @pl.when(at >= pl.num_programs(0) // 2)
    def _():
        fill(theirs_ref[...])


def project(mine, theirs, stacks, places, bias, factor, after):
    count, width = mine.shape
    columns = bias.shape[1]
    tile = 512
    each = count // tile
    whole = lambda shape: pl.BlockSpec(shape, lambda m, *_: (0,) * len(shape))
    tables = [jnp.stack([p[axis] for p in places]).astype(jnp.int32) for axis in range(2)]
    return pl.pallas_call(
        functools.partial(project_kernel, len(after)),
        grid_spec=pltpu.PrefetchScalarGridSpec(
            num_scalar_prefetch=2,
            grid=(2 * each,),
            in_specs=[
                pl.BlockSpec((tile, width), lambda m, *_: (jnp.minimum(m, each - 1), 0)),
                pl.BlockSpec((tile, width), lambda m, *_: (jnp.maximum(m - each, 0), 0)),
                whole((1, columns)),
                whole((1, columns)),
            ]
            + [whole(stack.shape) for stack in stacks]
            + [pl.BlockSpec(memory_space=pl.ANY)] * len(after),
            out_specs=[
                pl.BlockSpec((tile, columns), lambda m, *_: (m, 0)),
                whole((width, columns)),
            ],
        ),
        out_shape=[jax.ShapeDtypeStruct((2 * count, columns), BF16), jax.ShapeDtypeStruct((width, columns), BF16)],
        compiler_params=pltpu.CompilerParams(vmem_limit_bytes=44 * 1024 * 1024),
        cost_estimate=weight_of(11),
        name="project",
    )(*tables, *[mine, theirs, bias, factor, *stacks], *after)


def gelu_and_slope(u):
    d = 1.0 + (0.3275911 * 0.5**0.5) * jnp.abs(u)
    t = pl.reciprocal(d, approx=True).astype(BF16)
    e = jnp.exp2(u * u * (-0.5 * math.log2(math.e))).astype(BF16)
    u = u.astype(BF16)
    a = jnp.abs(u)
    low = lambda value: jnp.asarray(value, BF16)
    series = low(0.5 * 1.061405429) * t - low(0.5 * 1.453152027)
    series = series * t + low(0.5 * 1.421413741)
    series = series * t - low(0.5 * 0.284496736)
    series = series * t + low(0.5 * 0.254829592)
    tail = series * t * e
    active = jnp.maximum(u, low(0.0)) - a * tail
    below = tail - a * (e * low(1.0 / math.sqrt(2.0 * math.pi)))
    return active, jnp.where(u >= low(0.0), low(1.0) - below, below)


def total_rows(value):
    return jnp.sum(value, axis=0, keepdims=True)


def in_parts(count, work):
    def turn(at, carry):
        work(pl.ds(pl.multiple_of(at * 128, 128), 128))
        return carry

    lax.fori_loop(0, count // 128, turn, 0)


def ffn_kernel(
    count_of,
    core_ref,
    row_ref,
    part_ref,
    mine_ref,
    theirs_ref,
    rows_ref,
    cotan_ref,
    vec_ref,
    *more,
):
    stacks, more = more[:count_of], more[count_of:]
    active_ref, slope_ref, inner_out_ref, outer_w_ref, hidden_ref, normed_ref = more[:6]
    scale_ref, result_ref, grad_ref, out_w_ref, sums_ref, resid, acc, pre, inner_w, sems = more[6:]
    w, last = pl.program_id(0), pl.num_programs(0) - 1
    count, width = acc.shape
    chunk = pre.shape[2]
    vec = lambda at: vec_ref[at : at + 1, :]
    half_of = lambda at: out_w_ref[pl.ds(pl.multiple_of(at * (width // 2), width // 2), width // 2), :]
    slots = [(stack, k) for stack in stacks for k in range(stack.shape[0])]
    deep = 4 * width // len(slots)
    thin = width // len(slots)

    def fetch(block):
        for slot, (stack, k) in enumerate(slots):

            @pl.when(part_ref[slot] == block)
            def _():
                start = pl.multiple_of(row_ref[slot] * deep, deep)
                pltpu.make_async_copy(
                    stack.at[k, pl.ds(0, deep), :],
                    inner_w.at[lax.rem(block, 2), pl.ds(start, deep), :],
                    sems.at[lax.rem(block, 2)],
                ).start()

    def fetch_outer(block):
        for slot, (stack, k) in enumerate(slots):

            @pl.when(row_ref[slot] // 2 == block)
            def _():
                start = lax.rem(row_ref[slot], 2) * 4 * deep + part_ref[slot] * deep
                pltpu.make_async_copy(
                    stack.at[k, pl.ds(stack.shape[1] - deep, deep), :],
                    outer_w_ref.at[pl.ds(pl.multiple_of(start, deep), deep), :],
                    sems.at[3],
                ).start()

    def arrived(block):
        target = inner_w.at[lax.rem(block, 2)]
        pltpu.make_async_copy(target, target, sems.at[lax.rem(block, 2)]).wait()

    @pl.when(w == 0)
    def _():
        for slot, (stack, k) in enumerate(slots):
            start = pl.multiple_of(row_ref[slot] * 4 * thin + part_ref[slot] * thin, thin)
            pltpu.make_async_copy(
                stack.at[k, pl.ds(deep, thin), :], out_w_ref.at[pl.ds(start, thin), :], sems.at[2]
            ).start()
        fetch(w)
        pltpu.make_async_copy(out_w_ref, out_w_ref, sems.at[2]).wait()
        acc[...] = jnp.dot(mine_ref[...], half_of(core_ref[0]), preferred_element_type=F32)
        acc[...] += jnp.dot(theirs_ref[...], half_of(1 - core_ref[0]), preferred_element_type=F32)

        def enter(part):
            normed, scale = normalize(acc[part, :] + vec(2) + rows_ref[part, :].astype(F32))
            normed_ref[part, :] = normed.astype(BF16)
            scale_ref[part, :] = scale
            hidden = normed * vec(3) + vec(4)
            resid[part, :] = hidden + vec(5)
            hidden_ref[part, :] = hidden.astype(BF16)

        in_parts(count, enter)

    fetch_outer(w)
    arrived(w)

    @pl.when(w < last)
    def _():
        fetch(w + 1)

    now = lax.rem(w, 2)
    inner_out_ref[...] = inner_w[now]
    bias = vec_ref[pl.ds(8 + w, 1), :]

    def expand(n):
        cut = slice(n * chunk, (n + 1) * chunk)
        weight = inner_w[now, :, cut]
        pre[n % 2] = jnp.dot(hidden_ref[...], weight, preferred_element_type=F32)

    def bend(n):
        cut = slice(n * chunk, (n + 1) * chunk)
        for at in range(0, count, TILE):
            part = slice(at, at + TILE)
            active, slope = gelu_and_slope(pre[n % 2, part, :] + bias[:, cut])
            active_ref[part, cut] = active.astype(BF16)
            slope_ref[part, cut] = slope.astype(BF16)

    chunks = width // chunk
    expand(0)
    for n in range(1, chunks):
        expand(n)
        bend(n - 1)
    bend(chunks - 1)
    pltpu.make_async_copy(outer_w_ref, outer_w_ref, sems.at[3]).wait()

    def contract():
        weight = outer_w_ref[...]
        return jnp.dot(active_ref[...], weight, preferred_element_type=F32)

    @pl.when(w == 0)
    def _():
        acc[...] = contract()

    @pl.when(w > 0)
    def _():
        acc[...] += contract()

    @pl.when(w == last)
    def _():
        sums_ref[...] = jnp.zeros_like(sums_ref)

        def leave(part):
            normed, scale = normalize(resid[part, :] + acc[part, :])
            result_ref[part, :] = (normed * vec(6) + vec(7)).astype(BF16)
            cotan = cotan_ref[part, :].astype(F32)
            grad = norm_back(cotan * vec(6), normed, scale).astype(BF16)
            grad_ref[part, :] = grad
            sums_ref[0:1, :] += total_rows(cotan * normed)
            sums_ref[1:2, :] += total_rows(cotan)
            sums_ref[2:3, :] += total_rows(grad.astype(F32))

        in_parts(count, leave)


def ffn_back_kernel(
    core_ref,
    grad_ref,
    slope_ref,
    normed_ref,
    scale_ref,
    vec_ref,
    out_w_ref,
    inner_w_ref,
    outer_w_ref,
    after_ref,
    pre_grad_ref,
    branch_ref,
    mine_ref,
    theirs_ref,
    sums_ref,
    acc,
    pre,
):
    w = pl.program_id(0)
    count, width = acc.shape
    chunk = pre.shape[2]
    vec = lambda at: vec_ref[at : at + 1, :]

    @pl.when(w == 0)
    def _():
        sums_ref[...] = jnp.zeros_like(sums_ref)

    def pull(n):
        weight = outer_w_ref[n * chunk : (n + 1) * chunk, :]
        pre[n % 2] = lax.dot_general(grad_ref[...], weight, NT, preferred_element_type=F32)

    def bend(n):
        cut = slice(n * chunk, (n + 1) * chunk)
        sums = jnp.zeros((8, chunk), F32)
        for at in range(0, count, TILE):
            part = slice(at, at + TILE)
            back = pre[n % 2, part, :].astype(BF16).astype(F32) * slope_ref[part, cut].astype(F32)
            back = back.astype(BF16)
            pre_grad_ref[part, cut] = back
            sums += jnp.sum(back.astype(F32).reshape(TILE // 8, 8, chunk), axis=0)
        sums_ref[pl.ds(4 + w, 1), cut] += total_rows(sums)

    chunks = width // chunk
    pull(0)
    for n in range(1, chunks):
        pull(n)
        bend(n - 1)
    bend(chunks - 1)

    def contract():
        weight = inner_w_ref[...]
        return lax.dot_general(pre_grad_ref[...], weight, NT, preferred_element_type=F32)

    @pl.when(w == 0)
    def _():
        acc[...] = contract()

    @pl.when(w > 0)
    def _():
        acc[...] += contract()

    @pl.when(w == pl.num_programs(0) - 1)
    def _():
        def leave(part):
            through = acc[part, :].astype(BF16).astype(F32) + grad_ref[part, :].astype(F32)
            normed = normed_ref[part, :].astype(F32)
            branch = norm_back(through * vec(3), normed, scale_ref[part, :]).astype(BF16)
            branch_ref[part, :] = branch
            sums_ref[0:1, :] += total_rows(through * normed)
            sums_ref[1:2, :] += total_rows(through)
            sums_ref[2:3, :] += total_rows(branch.astype(F32))

        in_parts(count, leave)
        part = width // 2
        for out, at in ((mine_ref, core_ref[0]), (theirs_ref, 1 - core_ref[0])):
            weight = out_w_ref[pl.ds(pl.multiple_of(at * part, part), part), :]
            out[...] = lax.dot_general(
                branch_ref[...], weight, NT, preferred_element_type=F32
            ).astype(BF16)


def ffn_call(kernel, scalars, ins, anys, outs, scratch, width, steps, room, name):
    def spec(shape):
        if shape[1] == steps * width:
            return pl.BlockSpec((shape[0], width), lambda w: (0, w))
        if shape[0] == steps * width:
            return pl.BlockSpec((width, width), lambda w: (w, 0))
        return pl.BlockSpec(shape, lambda w: (0, 0), pipeline_mode=pl.Buffered(1))

    return pl.pallas_call(
        kernel,
        grid=(steps,),
        in_specs=[pl.BlockSpec(memory_space=pltpu.SMEM)] * len(scalars)
        + [spec(a.shape) for a in ins]
        + [pl.BlockSpec(memory_space=pl.ANY)] * len(anys),
        out_specs=[spec(shape) for shape, kind in outs],
        out_shape=[jax.ShapeDtypeStruct(shape, kind) for shape, kind in outs],
        scratch_shapes=scratch,
        compiler_params=pltpu.CompilerParams(vmem_limit_bytes=room * 1024 * 1024),
        cost_estimate=weight_of(40),
        name=name,
    )(*scalars, *ins, *anys)


def ffn(core, places, mine, theirs, rows, cotan, vec, stacks):
    count, width = rows.shape
    units = 4 * width
    low = (rows.shape, BF16)
    outs = [((count, units), BF16)] * 2 + [((width, units), BF16), ((units, width), BF16)]
    outs += [low, low, ((count, 1), F32), low, low, ((width, width), BF16), ((8, width), F32)]
    scratch = [
        pltpu.VMEM((count, width), F32),
        pltpu.VMEM((count, width), F32),
        pltpu.VMEM((2, count, 256), F32),
        pltpu.VMEM((2, width, width), BF16),
        pltpu.SemaphoreType.DMA((4,)),
    ]
    tables = [jnp.stack([p[axis] for p in places]).astype(jnp.int32) for axis in range(2)]
    kernel = functools.partial(ffn_kernel, len(stacks))
    ins = [mine, theirs, rows, cotan, vec]
    return ffn_call(kernel, [core, *tables], ins, stacks, outs, scratch, width, 4, 58, "ffn")


def ffn_back(core, grad, slope, normed, scale, vec, out_w, inner_w, outer_w, after):
    count, width = grad.shape
    part = ((count, width // 2), BF16)
    outs = [(slope.shape, BF16), (grad.shape, BF16), part, part, ((8, width), F32)]
    scratch = [pltpu.VMEM((count, width), F32), pltpu.VMEM((2, count, 256), F32)]
    ins = [grad, slope, normed, scale, vec, out_w, inner_w, outer_w]
    return ffn_call(
        ffn_back_kernel, [core], ins, after, outs, scratch, width, 4, 44, "ffn_back"
    )


def product_kernel(count, stacked, after, where_ref, *refs):
    lefts, right_ref, out_ref = refs[:count], refs[count], refs[count + 1 + after]
    if not stacked:
        total, rows = None, lefts[0].shape[0]
        for n, left_ref in enumerate(lefts):
            right = right_ref[n * rows : (n + 1) * rows, :]
            part = lax.dot_general(left_ref[...], right, TN, preferred_element_type=F32)
            total = part if n == 0 else total + part
        out_ref[...] = total.astype(BF16)
        return
    for n, left_ref in enumerate(lefts):

        @pl.when(pl.program_id(0) == n)
        def _():
            out_ref[...] = lax.dot_general(
                left_ref[...], right_ref[...], TN, preferred_element_type=F32
            ).astype(BF16)


def product(where, lefts, right, side, after=(), stacked=False):
    width = right.shape[1] // (1 if side is None else 2)
    tile = 512
    height = sum(left.shape[1] for left in lefts) if stacked else lefts[0].shape[1]
    micros = 2e-9 * height * width * right.shape[0] + 1
    half = lambda a, w: (0, 0 if side is None else (w[3] if side else 1 - w[3]))
    if stacked:
        left_place = lambda a, w: (0, 0)
        place = lambda a, w: (a + w[3] - 2 * a * w[3], 0)
    else:
        left_place = lambda a, w: (0, a)
        place = lambda a, w: (a, 0)
    return pl.pallas_call(
        functools.partial(product_kernel, len(lefts), stacked, len(after)),
        grid_spec=pltpu.PrefetchScalarGridSpec(
            num_scalar_prefetch=1,
            grid=(height // tile,),
            in_specs=[pl.BlockSpec((left.shape[0], tile), left_place) for left in lefts]
            + [pl.BlockSpec((right.shape[0], width), half, pipeline_mode=pl.Buffered(1))]
            + [pl.BlockSpec(memory_space=pl.ANY)] * len(after),
            out_specs=pl.BlockSpec((tile, width), place),
        ),
        out_shape=jax.ShapeDtypeStruct((height, width), BF16),
        compiler_params=pltpu.CompilerParams(vmem_limit_bytes=2 * SMALL_VMEM),
        cost_estimate=weight_of(micros),
        name="product",
    )(where, *[*lefts, right], *after)


def attend_kernel(held, seg_row_ref, seg_col_ref, qkv_ref, *rest):
    rest = rest[held:]
    out_refs, (lse_ref, bias_ref, stat_ref, score_ref, expo_ref) = rest[:2], rest[2:]
    half = qkv_ref.shape[2]
    pair = pl.program_id(1)
    length = bias_ref.shape[0]
    chunk = score_ref.shape[1]

    @pl.when(pair == 0)
    def _():
        bias_ref[...] = jnp.where(seg_col_ref[0] == seg_row_ref[0], 0.0, MASKED)
        stat_ref[...] = jnp.zeros_like(stat_ref)

    block = qkv_ref[:, 0].reshape(length, 3 * PAIR)
    q, k, v = (block[:, i * PAIR : (i + 1) * PAIR] for i in range(3))
    lane = lax.broadcasted_iota(jnp.int32, (length, PAIR), 1)
    low = lane < HD
    zero, one = jnp.zeros_like(q), jnp.ones_like(v)
    q_heads = [jnp.where(low, q, zero), jnp.where(low, zero, q)]
    v_heads = [jnp.where(low, v, one), jnp.where(low, one, v)]
    lane, low = lane[:chunk], low[:chunk]

    def score(step):
        c, h = divmod(step, 2)
        score_ref[step % 2] = lax.dot_general(
            q_heads[h][c * chunk : (c + 1) * chunk], k, NT, preferred_element_type=F32
        )

    def soften(step):
        c, h = divmod(step, 2)
        tops = []
        for at in range(0, chunk, TILE):
            rows = slice(c * chunk + at, c * chunk + at + TILE)
            s = score_ref[step % 2, at : at + TILE, :] + bias_ref[rows, :]
            top = jnp.max(s, axis=1, keepdims=True)
            expo_ref[step % 2, at : at + TILE, :] = jnp.exp(s - top).astype(BF16)
            tops.append(top)
        return jnp.concatenate(tops, 0)

    def mix(step):
        return jnp.dot(expo_ref[step % 2], v_heads[step % 2], preferred_element_type=F32)

    def finish(c, got, tops):
        rows = slice(c * chunk, (c + 1) * chunk)
        total = jnp.where(low, got[1], got[0])
        mixed = jnp.where(low, got[0], got[1]) / pltpu.roll(total, HD, 1)
        log = jnp.log(total)
        stat = stat_ref[rows, :]
        stat = jnp.where(lane == 2 * pair, tops[0] + log[:, HD : HD + 1], stat)
        stat_ref[rows, :] = jnp.where(lane == 2 * pair + 1, tops[1] + log[:, :1], stat)
        part, at = divmod(c * chunk, half)
        out_refs[part][0, at : at + chunk, :] = mixed.astype(BF16)

    steps = 2 * length // chunk
    tops, got = [], []
    score(0)
    for step in range(steps):
        if step + 1 < steps:
            score(step + 1)
        tops.append(soften(step))
        got.append(mix(step))
        if step % 2:
            finish(step // 2, got[-2:], tops[-2:])

    @pl.when(pair == pl.num_programs(1) - 1)
    def _():
        lse_ref[0] = jnp.transpose(stat_ref[...])[: lse_ref.shape[1]]


def attend_back_kernel(first_pair, after, *refs):
    seg_row_ref, seg_col_ref, qkv_ref, out_a, out_b, grad_a, grad_b, lse_ref = refs[:8]
    dqkv_ref, sums_ref, bias_ref, ds_ref, score_ref, slope_ref, prob_ref = refs[8 + after :]
    pair = pl.program_id(1)
    length = bias_ref.shape[0]
    half = qkv_ref.shape[2]
    chunk = score_ref.shape[1]

    @pl.when(pair == 0)
    def _():
        bias_ref[...] = jnp.where(seg_col_ref[0] == seg_row_ref[0], 0.0, MASKED)

    @pl.when((pair == 0) & (pl.program_id(0) == 0))
    def _():
        sums_ref[...] = jnp.zeros_like(sums_ref)

    block = qkv_ref[:, 0].reshape(length, 3 * PAIR)
    q, k, v = (block[:, i * PAIR : (i + 1) * PAIR] for i in range(3))
    out = jnp.concatenate([out_a[0], out_b[0]], 0)
    grad = jnp.concatenate([grad_a[0], grad_b[0]], 0)
    low = lax.broadcasted_iota(jnp.int32, (length, PAIR), 1) < HD
    zero = jnp.zeros_like(q)
    heads = lambda array: [jnp.where(low, array, zero), jnp.where(low, zero, array)]
    q_heads, k_heads, g_heads = heads(q), heads(k), heads(grad)
    product = jnp.transpose(out.astype(F32) * grad.astype(F32))
    chunks = length // chunk
    deltas = [total_rows(product[h * HD : (h + 1) * HD]) for h in range(2)]
    stats = [lse_ref[0, pl.ds(2 * (first_pair + pair) + h, 1), :] for h in range(2)]

    def score(step):
        h, c = divmod(step, chunks)
        rows = slice(c * chunk, (c + 1) * chunk)
        score_ref[step % 2] = lax.dot_general(k[rows], q_heads[h], NT, preferred_element_type=F32)
        slope_ref[step % 2] = lax.dot_general(v[rows], g_heads[h], NT, preferred_element_type=F32)

    def bend(step):
        h, c = divmod(step, chunks)
        for at in range(0, chunk, TILE):
            rows = slice(c * chunk + at, c * chunk + at + TILE)
            part = slice(at, at + TILE)
            p = jnp.exp(score_ref[step % 2, part, :] + bias_ref[rows, :] - stats[h])
            prob_ref[step % 2, part, :] = p.astype(BF16)
            ds_ref[h, rows, :] = (p * (slope_ref[step % 2, part, :] - deltas[h])).astype(BF16)

    steps = 2 * chunks
    dk, dv = [None] * chunks, [None] * chunks
    dq = None
    score(0)
    for step in range(steps):
        h, c = divmod(step, chunks)
        if step + 1 < steps:
            score(step + 1)
        bend(step)
        rows = slice(c * chunk, (c + 1) * chunk)
        v_part = jnp.dot(prob_ref[step % 2], g_heads[h], preferred_element_type=F32)
        k_part = jnp.dot(ds_ref[h, rows, :], q_heads[h], preferred_element_type=F32)
        if h == 0:
            dk[c], dv[c] = k_part, v_part
        else:
            part, at = c * chunk // half, c * chunk % half
            dqkv_ref[part, 0, at : at + chunk, PAIR : 2 * PAIR] = (dk[c] + k_part).astype(BF16)
            dv[c] = (dv[c] + v_part).astype(BF16)
            dqkv_ref[part, 0, at : at + chunk, 2 * PAIR :] = dv[c]
        if c == chunks - 1:
            part = lax.dot_general(ds_ref[h], k_heads[h], TN, preferred_element_type=F32)
            dq = part if h == 0 else dq + part
    dq = (dq * HD**-0.5).astype(BF16)
    dqkv_ref[:, 0, :, :PAIR] = dq.reshape(-1, half, PAIR)
    sums = [total_rows(dq.astype(F32)), sum(total_rows(part.astype(F32)) for part in dv)]
    sums_ref[0:1, pl.ds(pl.multiple_of(pair * PAIR, PAIR), PAIR)] += sums[0]
    sums_ref[1:2, pl.ds(pl.multiple_of(pair * PAIR, PAIR), PAIR)] += sums[1]


def attention_call(
    kernel, seg, arrays, pairs, outs, scratch, name, first=0, after=(), seqs=None, held=()
):
    parts, count, half, columns = arrays[0].shape
    start, seqs = seqs or (0, count)
    micros = 6.5 * seqs if name == "attend" else 3.7 * seqs
    length = parts * half

    def spec(array, first):
        shape = array.shape
        if len(shape) == 4:
            return pl.BlockSpec(
                (parts, 1, half, 3 * PAIR), lambda s, p: (0, start + s, 0, first + p)
            )
        if len(shape) == 3 and shape[1] == half:
            return pl.BlockSpec((1, half, PAIR), lambda s, p: (start + s, 0, first + p))
        if len(shape) == 3:
            return pl.BlockSpec((1,) + shape[1:], lambda s, p: (start + s, 0, 0))
        return pl.BlockSpec(shape, lambda s, p: (0, 0))

    operands = [seg[:, None, :], seg[:, :, None]] + arrays
    return pl.pallas_call(
        kernel,
        grid=(seqs, pairs),
        in_specs=[spec(a, first) for a in operands]
        + [pl.BlockSpec(memory_space=pl.ANY)] * (len(held) + len(after)),
        out_specs=[spec(a, 0) for a in outs],
        out_shape=outs,
        scratch_shapes=scratch(length),
        input_output_aliases={len(operands) + n: n for n in range(len(held))},
        compiler_params=pltpu.CompilerParams(vmem_limit_bytes=SMALL_VMEM),
        cost_estimate=weight_of(micros),
        name=name,
    )(*operands, *held, *after)


def attend(qkv, seg, seqs, held, after):
    parts, count, half, columns = qkv.shape
    pairs = columns // (3 * PAIR)
    outs = [
        jax.ShapeDtypeStruct((count, half, columns // 3), BF16),
        jax.ShapeDtypeStruct((count, half, columns // 3), BF16),
        jax.ShapeDtypeStruct((count, 2 * pairs, parts * half), F32),
    ]
    scratch = lambda length: [
        pltpu.VMEM((length, length), F32),
        pltpu.VMEM((length, PAIR), F32),
        pltpu.VMEM((2, 128, length), F32),
        pltpu.VMEM((2, 128, length), BF16),
    ]
    kernel = functools.partial(attend_kernel, len(held) + len(after))
    return attention_call(
        kernel, seg, [qkv], pairs, outs, scratch, "attend", 0, after, seqs, held
    )


def attend_back(qkv, seg, out, grad, lse, first, pairs, after):
    outs = [
        jax.ShapeDtypeStruct(qkv.shape[:3] + (3 * PAIR * pairs,), BF16),
        jax.ShapeDtypeStruct((8, PAIR * pairs), F32),
    ]
    scratch = lambda length: [
        pltpu.VMEM((length, length), F32),
        pltpu.VMEM((2, length, length), BF16),
        pltpu.VMEM((2, 128, length), F32),
        pltpu.VMEM((2, 128, length), F32),
        pltpu.VMEM((2, 128, length), BF16),
    ]
    kernel = functools.partial(attend_back_kernel, first, len(after))
    arrays = [qkv, *out, *grad, lse]
    return attention_call(kernel, seg, arrays, pairs, outs, scratch, "attend_back", first, after)


def body(
    layer_input,
    segment_ids,
    out_cotangent,
    attn_master,
    inner_master,
    outer_master,
    vector_master,
    attn_moment,
    inner_moment,
    outer_moment,
    vector_moment,
    attn_square,
    inner_square,
    outer_square,
    vector_square,
):
    seqs, half, width = layer_input.shape
    count = seqs * half
    hidden_units = inner_master.shape[1]
    pairs = width // (2 * PAIR)
    part_cols = width // 2
    shards = lax.axis_size("shard")
    owned_rows = attn_master.shape[1]
    core = lax.axis_index("ctx")
    first = core == 0

    def own_half(array, axis):
        size = array.shape[axis] // 2
        return lax.dynamic_slice_in_dim(array, core * size, size, axis)

    def other_half(array, axis):
        size = array.shape[axis] // 2
        return lax.dynamic_slice_in_dim(array, (1 - core) * size, size, axis)

    def in_order(mine, theirs, axis):
        return jnp.concatenate(
            [jnp.where(first, mine, theirs), jnp.where(first, theirs, mine)], axis
        )

    rows = layer_input.reshape(count, width)
    rows_theirs = swap_cores(rows)
    square = is_square()
    o, i, y, inner = position()
    where = jnp.stack([o, i, y, core]).astype(jnp.int32)

    piece = own_half(attn_master[:3], 2).astype(BF16).reshape(3, owned_rows, pairs, PAIR)
    piece = piece.transpose(1, 2, 0, 3).reshape(owned_rows, 3 * part_cols)
    vec_low = vector_master.astype(BF16)
    rider = vec_low[:2].reshape(1, -1)
    if square:
        piece = lax.dynamic_slice_in_dim(piece, y * (piece.shape[1] // 2), piece.shape[1] // 2, 1)
    rider = jnp.pad(rider, ((0, 15), (0, piece.shape[1] - rider.shape[1])))
    piece = jnp.concatenate([piece, rider], 0)

    def every_row(block):
        size = block.shape[0] // (lax.axis_size("replica") * 2)
        part = lax.dynamic_slice_in_dim(block, (2 * y + core) * size, size, 0).astype(BF16)
        return lax.all_gather(part, EVERY, axis=0, tiled=True)

    def placed(found, slots):
        chosen = jnp.stack([place[0] for place in slots[:shards]])
        chosen = (jnp.arange(shards)[:, None] == chosen[None, :]).astype(F32)
        return jnp.einsum("ps,srw->rpw", chosen, found.astype(F32)).reshape(-1, width)

    if square:
        q = 2 * core + y
        vec_rows = jnp.pad(vec_low.reshape(-1), (0, 16 * width - vec_low.size)).reshape(16, width)
        quarter = jnp.concatenate(
            [
                lax.dynamic_slice_in_dim(inner_master, q * width, width, 1).astype(BF16),
                lax.dynamic_slice_in_dim(
                    attn_master[3], q * (owned_rows // 4), owned_rows // 4, 0
                ).astype(BF16),
                vec_rows,
                lax.dynamic_slice_in_dim(
                    outer_master, q * (outer_master.shape[0] // 4), outer_master.shape[0] // 4, 0
                ).astype(BF16),
            ],
            0,
        )
        line = jnp.stack([piece] + [shift_outer(piece, -k) for k in range(1, OUTER)])
        near_x, near_y = shift_inner(line, 1), shift_replica(line, 1)
        (quarter,) = relay(where, [quarter], (line,))
        across = swap_outer(quarter, 2)
        two = (OUTER // 2,)
        far = small_call(
            halves_kernel, where, [near_x, near_y], [two + piece.shape] * 2, (), "halves"
        )
        stacks = [line, near_x, near_y, shift_inner(far[0], 1), shift_replica(far[1], 1)]
        (pair,) = small_call(
            pair_kernel, where, [quarter, across], [two + quarter.shape], tuple(stacks[3:]), "pair"
        )
        places = quarter_places([lax.rem(o + k, OUTER) for k in range(OUTER)])
        other_pair = swap_outer(pair, 1)
        pair_x, pair_y = shift_inner(pair, 1), shift_replica(pair, 1)
        done = (pair,)
    else:
        stacks = [item[None] for item in ring_gather(piece)]
        places = [(owner, 0) for owner in slot_owners()]
        wide = hidden_units // width
        inner_w = every_row(inner_master).reshape(8, -1, wide, width).transpose(0, 2, 1, 3)
        slots = [inner_w.reshape(PARTS, -1, width), every_row(attn_master[3]).reshape(PARTS, -1, width)]
        slots = jnp.pad(jnp.concatenate(slots, 1), ((0, 0), (0, 16), (0, 0)))
        outer_w = every_row(outer_master).reshape(PARTS, -1, width)
        slots = jnp.concatenate([slots, outer_w], 1)
        wide_stacks = [slots[n : n + 2] for n in range(0, PARTS, 2)]
        wide_places = [(jnp.int32(n // 4), jnp.int32(n % 4)) for n in range(PARTS)]
        vec = lax.all_gather(vec_low, "shard", axis=1, tiled=True).astype(F32)
        done = ()
    riders = jnp.concatenate([stack[:, owned_rows] for stack in stacks], 0)[:shards]
    riders = riders[:, : 2 * width // shards].reshape(shards, 2, -1)
    biases = placed(riders, places)

    halves = own_half(biases, 1).reshape(2, pairs, PAIR)
    bias = jnp.stack([halves[0], jnp.zeros_like(halves[0]), halves[1]], 1).reshape(1, -1)
    ones = jnp.ones((pairs, PAIR), F32)
    factor = jnp.stack([ones * HD**-0.5, ones, ones], 1).reshape(1, -1)
    qkv, qkv_w = project(rows, rows_theirs, stacks, places, bias, factor, done)
    qkv = qkv.reshape(2, seqs, half, 3 * part_cols)
    seg = jnp.concatenate([own_half(segment_ids, 1), other_half(segment_ids, 1)], 1)
    if square:
        (other_pair,) = relay(where, [other_pair], (qkv_w,))
        other_x, other_y = shift_inner(other_pair, 1), shift_replica(other_pair, 1)
        early = attend(qkv, seg, (0, seqs // 2), (), (other_pair,))
        near = [pair, other_pair, pair_x, other_x, pair_y, other_y]
        bulk, *relayed = small_call(
            bulk_kernel,
            where,
            near,
            [(12,) + quarter.shape, pair.shape, pair.shape],
            (early[0],),
            "bulk",
        )
        far_pair = [shift_inner(relayed[0], 1), shift_replica(relayed[1], 1)]
        near_rows = bulk[:8, 160:162].reshape(shards, -1)[:, : vec_low.size]
        both = line_order(o)
        places = quarter_places(both[0] + both[1])
        vec = placed(near_rows.reshape((shards,) + vec_low.shape), places)
        wide_places = [(row, 2 * core + side) for row, side in places]
        wide_places += [(row, 2 * (1 - core) + side) for row, side in places]
    else:
        early = attend(qkv, seg, (0, seqs // 2), (), ())
    mixed_mine, mixed_sent, lse = attend(qkv, seg, (seqs // 2, seqs - seqs // 2), early, ())
    if square:
        (far_bulk,) = small_call(
            bulk_kernel, where, far_pair, [(4,) + quarter.shape], (mixed_mine,), "bulk"
        )
        wide_stacks = [bulk, far_bulk, swap_cores(bulk), swap_cores(far_bulk)]
    flat = lambda array: array.reshape(count, part_cols)
    deep = lambda array: array.reshape(seqs, half, part_cols)
    heads_mine, heads_theirs = flat(mixed_mine), swap_cores(flat(mixed_sent))

    cotan = out_cotangent.reshape(count, width)
    core_at = jnp.full((1,), core, jnp.int32)
    forward = ffn(core_at, wide_places, heads_mine, heads_theirs, rows, cotan, vec, wide_stacks)
    active, slope, inner_w, outer_w, hidden_low, normed, scale, result = forward[:8]
    ffn_grad, out_w, sums_two = forward[8:]

    by_shard = lambda array: array.reshape(shards, -1, array.shape[1])

    outer_sent = product(where, [active], ffn_grad, 0)
    outer_kept = product(where, [active], ffn_grad, 1, (outer_sent,))
    outer_chips = [by_shard(outer_kept), by_shard(swap_cores(outer_sent))]
    done = (outer_kept,)
    if square:
        outer = Sum(where, outer_chips)
        done = outer.merge()
    pre_grad, branch_grad, mine, sent, sums_one = ffn_back(
        core_at, ffn_grad, slope, normed, scale, vec, out_w, inner_w, outer_w, done[:1]
    )
    got = swap_cores(sent)
    mixed_grad = [deep(mine), deep(got)]
    done = outer.plane((pre_grad,)) if square else ()
    heads = [heads_mine, heads_theirs]
    inner_kept = product(where, [hidden_low], pre_grad, 1, done)
    done = outer.cross((inner_kept,)) if square else (inner_kept,)
    inner_sent = product(where, [hidden_low], pre_grad, 0, done)
    out_sent = product(where, heads, branch_grad, 0, (inner_sent,), True)
    out_kept = product(where, heads, branch_grad, 1, (out_sent,), True)
    inner_chips = [by_shard(inner_kept), by_shard(swap_cores(inner_sent))]
    out_chips = [by_shard(out_kept), by_shard(swap_cores(out_sent))]

    def back(first, after):
        grad, sums = attend_back(
            qkv, seg, (mixed_mine, mixed_sent), mixed_grad, lse, first, pairs // 2, after
        )
        return grad.reshape(2 * count, -1), sums

    def vector_chip(sums_a, sums_b):
        blank = jnp.zeros((part_cols,), F32)
        ours = jnp.concatenate([sums_a, sums_b], 1)
        attn_biases = jnp.stack([in_order(ours[at], blank, 0) for at in range(2)])
        sums = [attn_biases, sums_one[2:3], sums_one[:2], sums_two[2:3], sums_two[:2]]
        sums = jnp.concatenate(sums + [sums_one[4:8]], 0)
        sums = sums.reshape(-1, shards, width // shards).transpose(1, 0, 2)
        sums = jnp.pad(sums, ((0, 0), (0, owned_rows - sums.shape[1]), (0, 0)))
        return sums.astype(BF16)

    outer_states = (outer_master, outer_moment, outer_square)
    inner_states = (inner_master, inner_moment, inner_square)
    attn_states = (attn_master, attn_moment, attn_square)
    if square:
        inner = Sum(where, inner_chips)
        done = outer.turn((out_kept,))
        done = inner.merge(done)
        grad_a, sums_a = back(0, done)
        done = outer.line((grad_a,))
        ours = by_shard(product(where, [rows, rows_theirs], grad_a, None, done))
        done = inner.plane((ours,))
        sum_a = Sum(where, [ours], out_chips)
        done = sum_a.merge(done)
        grad_b, sums_b = back(pairs // 2, done)
        done = inner.cross((grad_b,))
        done = sum_a.plane(done)
        theirs_part = input_back(grad_a, grad_b, qkv_w, (), done)
        ours = by_shard(product(where, [rows, rows_theirs], grad_b, None, (theirs_part,)))
        sum_b = Sum(where, [ours], [vector_chip(sums_a, sums_b)])
        done = sum_a.cross((ours,))
        done = sum_b.merge(done)
        outer_new = update(where, outer_states, [outer.shares], done)
        input_grad = input_back(
            grad_a, grad_b, qkv_w, (branch_grad, swap_cores(theirs_part)), (outer_new[0],)
        )
        done = sum_b.plane((input_grad,))
        done = inner.turn(done)
        done = sum_a.turn(done)
        done = sum_b.cross(done)
        done = inner.line(done)
        done = sum_b.turn(done)
        inner_new = update(where, inner_states, [inner.shares], done)
        done = sum_a.line((inner_new[0],))
        sum_b.line(done)
        attn_shares = [sum_a.shares, sum_b.shares]
        vector_shares = [
            jnp.concatenate(
                [
                    jnp.where(y == 0, sum_b.shares[at], sum_b.shares[at + 1])[0],
                    jnp.where(y == 0, sum_b.shares[at + 1], sum_b.shares[at])[0],
                ],
                0,
            )
            for at in (0, 2)
        ]
    else:
        grad_a, sums_a = back(0, ())
        grad_b, sums_b = back(pairs // 2, ())
        theirs_part = input_back(grad_a, grad_b, qkv_w, (), ())
        added = (branch_grad, swap_cores(theirs_part))
        input_grad = input_back(grad_a, grad_b, qkv_w, added, ())
        outer_new = update(where, outer_states, [sum_apart(add_low(*outer_chips))])
        inner_new = update(where, inner_states, [sum_apart(add_low(*inner_chips))])
        ours = [by_shard(product(where, [rows, rows_theirs], grad, None)) for grad in (grad_a, grad_b)]
        chip_a = jnp.concatenate([ours[0], add_low(*out_chips)], 2)
        chip_b = jnp.concatenate([ours[1], vector_chip(sums_a, sums_b)], 2)
        attn_shares = [sum_apart(chip_a), sum_apart(chip_b)]
        vector_shares = [share[0] for share in attn_shares[1]]
    attn_new = update(where, attn_states, attn_shares)
    cut = grad_b.shape[1]
    vector_sum = sum(share[: vec_low.shape[0], cut:].astype(F32) for share in vector_shares)
    vector_new = adamw(vector_sum, vector_moment, vector_square, vector_master, RATE_VECTOR)
    vector_new = vector_new + (vector_new[2].astype(BF16),)
    news = (attn_new, inner_new, outer_new, vector_new)
    updates = [[new[at] for new in news] for at in range(4)]
    return (
        result.reshape(seqs, half, width).astype(BF16),
        input_grad.reshape(seqs, half, width),
        *[item for kind in updates for item in kind],
    )


def solution(mesh):
    tokens = P(("replica", "shard"), "ctx", None)
    states = (P(None, "shard", None), P("shard", None), P("shard", None), P(None, "shard"))
    in_specs = (tokens, P(("replica", "shard"), None), tokens) + states * 3
    out_specs = (tokens, tokens) + states * 4
    return jax.shard_map(body, mesh=mesh, in_specs=in_specs, out_specs=out_specs, check_vma=False)
```

profile of v0, /device:TPU:0, one launch (start us, length us, event | category | flops | bytes accessed | tf_op | source)
XLA Modules:
  0.0 498.9 jit_solution(9722535744041764154)
XLA Ops:
  2.8 5.1 %collective-permute-start.1 = (bf16[144,768]{1,0:T(8,128)(2,1)S(1)}, bf16[144,768]{1,0:T(8,128)(2,1)S(1)}, u32[]{:S(2)}, u32[]{:S(2)}) collective-permute-start(bf16[144,768]{1,0:T(8,128)(2,1)S(1)} %get-tuple-element.212), channel_id=1, source_target_pairs={{0,12},{2,14},{4,0},{6,2},{8,4},{10,6},{12,8},{14,10},{1,13},{3,15... | collective-permute-start | bytes 663560 | tf_op jit(solution)/shard_map/ppermute | solution.py:77
  8.9 4.9 collective-permute-done.1
  13.8 13.0 %collective-permute-done.2 = bf16[144,768]{1,0:T(8,128)(2,1)} collective-permute-done((bf16[144,768]{1,0:T(8,128)(2,1)S(1)}, bf16[144,768]{1,0:T(8,128)(2,1)}, u32[]{:S(2)}, u32[]{:S(2)}) %collective-permute-start.2) | collective-permute-done | bytes 221216 | tf_op jit(solution)/shard_map/ppermute | solution.py:77
  34.9 2.8 collective-permute-start.8
  37.6 11.7 %collective-permute-done.4.near_x.rest_1_ = bf16[4,144,768]{2,1,0:T(8,128)(2,1)} collective-permute-done((bf16[4,144,768]{2,1,0:T(8,128)(2,1)S(1)}, bf16[4,144,768]{2,1,0:T(8,128)(2,1)}, u32[]{:S(2)}, u32[]{:S(2)}) %collective-permute-start.4) | collective-permute-done | bytes 884768 | tf_op jit(solution)/shard_map/ppermute | solution.py:85
  54.2 9.7 %collective-permute-done.8.other = bf16[304,1024]{1,0:T(8,128)(2,1)S(1)} collective-permute-done((bf16[304,1024]{1,0:T(8,128)(2,1)S(1)}, bf16[304,1024]{1,0:T(8,128)(2,1)S(1)}, u32[]{:S(2)}, u32[]{:S(2)}) %collective-permute-start.8) | collective-permute-done | bytes 622624 | tf_op jit(solution)/shard_map/ppermute | solution.py:139
  70.8 12.0 %project.1 = (bf16[2048,1536]{1,0:T(8,128)(2,1)}, bf16[1024,1536]{1,0:T(8,128)(2,1)}) custom-call(s32[16]{0:T(128)S(1)} %stack.90.row_ref, s32[16]{0:T(128)S(1)} %stack.93.column_ref, bf16[1024,1024]{1,0:T(8,128)(2,1)S(1)} %bitcast.170, bf16[1024,1024]{1,0:T(8,128)(2,1)} %collective-permute-done.theirs_ref.refs_1_, f32[1,1536]{1,0:T(1,128)S(1)} %reshape.159.bias_ref, ...), custom_call_target="tpu_custom_call" | custom-call | flops 3190000128 | bytes 10120000 | tf_op jit(solution)/shard_map/project/pallas_call | solution.py:451
  82.8 12.2 %collective-permute-done.9.rest_0_ = bf16[2,304,1024]{2,1,0:T(8,128)(2,1)} collective-permute-done((bf16[2,304,1024]{2,1,0:T(8,128)(2,1)}, bf16[2,304,1024]{2,1,0:T(8,128)(2,1)}, u32[]{:S(2)}, u32[]{:S(2)}) %collective-permute-start.9) | collective-permute-done | bytes 1245216 | tf_op jit(solution)/shard_map/ppermute | solution.py:139
  101.1 2.8 copy-done.58
  103.9 13.9 %attend.2 = (bf16[4,256,512]{2,1,0:T(8,128)(2,1)S(1)}, bf16[4,256,512]{2,1,0:T(8,128)(2,1)}, f32[4,8,512]{2,1,0:T(8,128)S(1)}) custom-call(s32[4,1,512]{2,1,0:T(1,128)S(1)} %broadcast_in_dim.9.seg_row_ref.refs_0_, s32[4,512,1]{2,1,0:T(8,128)S(1)} %copy.63.seg_col_ref.refs_1_, bf16[2,4,256,1536]{3,2,1,0:T(8,128)(2,1)S(1)} %bitcast.181, ...), custom_call_target="tpu_custom_call" | custom-call | flops 3769999872 | bytes 11960000 | tf_op jit(solution)/shard_map/attend/pallas_call | solution.py:986
  117.8 8.8 %collective-permute-done.12.rest_3_ = bf16[2,304,1024]{2,1,0:T(8,128)(2,1)S(1)} collective-permute-done((bf16[2,304,1024]{2,1,0:T(8,128)(2,1)S(1)}, bf16[2,304,1024]{2,1,0:T(8,128)(2,1)S(1)}, u32[]{:S(2)}, u32[]{:S(2)}) %collective-permute-start.12) | collective-permute-done | bytes 1245216 | tf_op jit(solution)/shard_map/ppermute | solution.py:85
  127.0 6.1 %bulk.2 = (bf16[12,304,1024]{2,1,0:T(8,128)(2,1)}, bf16[2,304,1024]{2,1,0:T(8,128)(2,1)S(1)}, bf16[2,304,1024]{2,1,0:T(8,128)(2,1)S(1)}) custom-call(s32[4]{0:T(128)S(1)} %pad_add_fusion.1.where_ref, bf16[2,304,1024]{2,1,0:T(8,128)(2,1)} %pair.1.rest_5_.rest_0_, bf16[2,304,1024]{2,1,0:T(8,128)(2,1)S(1)} %relay.3.rest_0_.rest_1_, ...), custom_call_target="tpu_custom_call" | custom-call | flops 290000000 | bytes 920000 | tf_op jit(solution)/shard_map/bulk/pallas_call | solution.py:160
  135.1 13.9 %attend.3 = (bf16[4,256,512]{2,1,0:T(8,128)(2,1)S(1)}, bf16[4,256,512]{2,1,0:T(8,128)(2,1)}, f32[4,8,512]{2,1,0:T(8,128)S(1)}) custom-call(s32[4,1,512]{2,1,0:T(1,128)S(1)} %broadcast_in_dim.9.seg_row_ref.refs_0_, s32[4,512,1]{2,1,0:T(8,128)S(1)} %copy.63.seg_col_ref.refs_1_, ...), custom_call_target="tpu_custom_call", output_to_operand_aliasing={{0}: (3, {}), {1}: (4, {}), {2}: (5, {})} | custom-call | flops 3769999872 | bytes 11960000 | tf_op jit(solution)/shard_map/attend/pallas_call | solution.py:986
  149.0 13.9 %collective-permute-done.15.rest_0_ = bf16[2,304,1024]{2,1,0:T(8,128)(2,1)S(1)} collective-permute-done((bf16[2,304,1024]{2,1,0:T(8,128)(2,1)S(1)}, bf16[2,304,1024]{2,1,0:T(8,128)(2,1)S(1)}, u32[]{:S(2)}, u32[]{:S(2)}) %collective-permute-start.15) | collective-permute-done | bytes 1245216 | tf_op jit(solution)/shard_map/ppermute | solution.py:85
  168.5 2.5 collective-permute-done.10.theirs_ref.refs_1_
  171.9 50.7 %ffn.1 = (bf16[1024,4096]{1,0:T(8,128)(2,1)}, bf16[1024,4096]{1,0:T(8,128)(2,1)}, bf16[1024,4096]{1,0:T(8,128)(2,1)}, bf16[4096,1024]{1,0:T(8,128)(2,1)}, bf16[1...) custom-call(s32[1]{0:T(128)} %bitcast.core_ref, ...), custom_call_target="tpu_custom_call" | custom-call | flops 11600000000 | bytes 36800000 | tf_op jit(solution)/shard_map/ffn/pallas_call | solution.py:730
  222.6 3.4 copy-done.9
  227.6 7.3 %product.8.refs_2_ = bf16[4096,512]{1,0:T(8,128)(2,1)S(1)} custom-call(s32[4]{0:T(128)S(1)} %pad_add_fusion.1.where_ref, bf16[1024,4096]{1,0:T(8,128)(2,1)S(1)} %copy-done.9, bf16[1024,1024]{1,0:T(8,128)(2,1)S(1)} %copy-done.19), custom_call_target="tpu_custom_call" | custom-call | flops 1535540480 | bytes 4871369 | tf_op jit(solution)/shard_map/product/pallas_call | solution.py:806
  235.3 7.3 %product.9 = bf16[4096,512]{1,0:T(8,128)(2,1)S(1)} custom-call(s32[4]{0:T(128)S(1)} %pad_add_fusion.1.where_ref, bf16[1024,4096]{1,0:T(8,128)(2,1)S(1)} %copy-done.9, bf16[1024,1024]{1,0:T(8,128)(2,1)S(1)} %copy-done.19, bf16[4096,512]{1,0:T(8,128)(2,1)S(1)} %product.8.refs_2_), custom_call_target="tpu_custom_call" | custom-call | flops 1535540480 | bytes 4871369 | tf_op jit(solution)/shard_map/product/pallas_call | solution.py:806
  245.7 32.2 %ffn_back.1 = (bf16[1024,4096]{1,0:T(8,128)(2,1)}, bf16[1024,1024]{1,0:T(8,128)(2,1)S(1)}, bf16[1024,512]{1,0:T(8,128)(2,1)S(1)}, bf16[1024,512]{1,0:T(8,128)(2,1)S(1)}, f32[8,1024]{1,0:T(8,128)S(1)}) custom-call(s32[1]{0:T(128)} %bitcast.core_ref, bf16[1024,1024]{1,0:T(8,128)(2,1)S(1)} %copy-done.20, bf16[1024,4096]{1,0:T(8,128)(2,1)} %get-tuple-element.125.slope_ref, ...), custom_call_target="tpu_custom_call" | custom-call | flops 11600000000 | bytes 36800000 | tf_op jit(solution)/shard_map/ffn_back/pallas_call | solution.py:730
  278.9 4.1 copy-done.2
  287.3 5.7 %product.10.rest_0_ = bf16[1024,2048]{1,0:T(8,128)(2,1)S(1)} custom-call(s32[4]{0:T(128)S(1)} %pad_add_fusion.1.where_ref, bf16[1024,1024]{1,0:T(8,128)(2,1)S(1)} %copy-done.15, bf16[1024,4096]{1,0:T(8,128)(2,1)S(1)} %copy-done.3, bf16[4,128,512]{2,1,0:T(8,128)(2,1)S(1)} %get-tuple-element.141.refs_2_, bf16[4,128,512]{2,1,0:T(8,128)(2,1)S(1)} %get-tuple-element.142.refs_3_), custom_call_target="tpu_custom_call" | custom-call | flops 1535540480 | bytes 4871369 | tf_op jit(solution)/shard_map/product/pallas_call | solution.py:806
  293.0 4.5 collective-permute-done.23.got_p
  299.7 7.3 %product.11.refs_3_ = bf16[1024,2048]{1,0:T(8,128)(2,1)} custom-call(s32[4]{0:T(128)S(1)} %pad_add_fusion.1.where_ref, bf16[1024,1024]{1,0:T(8,128)(2,1)S(1)} %copy-done.15, bf16[1024,4096]{1,0:T(8,128)(2,1)S(1)} %copy-done.3, bf16[2,2,128,512]{3,2,1,0:T(8,128)(2,1)S(1)} %get-tuple-element.145.refs_2_), custom_call_target="tpu_custom_call" | custom-call | flops 1535540480 | bytes 4871369 | tf_op jit(solution)/shard_map/product/pallas_call | solution.py:806
  307.6 2.1 product.12.refs_3_
  312.0 9.4 %collective-permute-done.26.got = bf16[2,2,128,512]{3,2,1,0:T(8,128)(2,1)S(1)} collective-permute-done((bf16[2,2,128,512]{3,2,1,0:T(8,128)(2,1)S(1)}, bf16[2,2,128,512]{3,2,1,0:T(8,128)(2,1)S(1)}, u32[]{:S(2)}, u32[]{:S(2)}) %collective-permute-start.26) | collective-permute-done | bytes 524320 | tf_op jit(solution)/shard_map/ppermute | solution.py:139
  326.2 15.1 %attend_back.2 = (bf16[2,4,256,768]{3,2,1,0:T(8,128)(2,1)S(1)}, f32[8,256]{1,0:T(8,128)S(1)}) custom-call(s32[4,1,512]{2,1,0:T(1,128)S(1)} %broadcast_in_dim.9.seg_row_ref.refs_0_, s32[4,512,1]{2,1,0:T(8,128)S(1)} %copy-done.36, bf16[2,4,256,1536]{3,2,1,0:T(8,128)(2,1)S(1)} %bitcast.185, bf16[4,256,512]{2,1,0:T(8,128)(2,1)S(1)} %copy-done.13, ...), custom_call_target="tpu_custom_call" | custom-call | flops 4292000000 | bytes 13616000 | tf_op jit(solution)/shard_map/attend_back/pallas_call | solution.py:986
  344.0 5.5 %product.14 = bf16[1024,768]{1,0:T(8,128)(2,1)S(1)} custom-call(s32[4]{0:T(128)S(1)} %pad_add_fusion.1.where_ref, bf16[1024,1024]{1,0:T(8,128)(2,1)S(1)} %bitcast.171, bf16[1024,1024]{1,0:T(8,128)(2,1)} %collective-permute-done.theirs_ref.refs_1_, bf16[2048,768]{1,0:T(8,128)(2,1)S(1)} %bitcast.149, bf16[2,128,512]{2,1,0:T(8,128)(2,1)S(1)} %fold_line.4.refs_3_), custom_call_target="tpu_custom_call" | custom-call | flops 1224155392 | bytes 3883527 | tf_op jit(solution)/shard_map/product/pallas_call | solution.py:806
  352.9 2.5 merge.6
  363.0 2.8 copy-done.60
  367.1 15.0 %attend_back.3 = (bf16[2,4,256,768]{3,2,1,0:T(8,128)(2,1)S(1)}, f32[8,256]{1,0:T(8,128)S(1)}) custom-call(s32[4,1,512]{2,1,0:T(1,128)S(1)} %broadcast_in_dim.9.seg_row_ref.refs_0_, s32[4,512,1]{2,1,0:T(8,128)S(1)} %copy-done.36, bf16[2,4,256,1536]{3,2,1,0:T(8,128)(2,1)S(1)} %bitcast.186, bf16[4,256,512]{2,1,0:T(8,128)(2,1)S(1)} %copy-done.13, ...), custom_call_target="tpu_custom_call" | custom-call | flops 4292000000 | bytes 13616000 | tf_op jit(solution)/shard_map/attend_back/pallas_call | solution.py:986
  382.1 3.0 collective-permute-done.33.got_p
  386.8 2.6 fold_plane.6
  389.4 5.4 %input_back.2.refs_3_ = bf16[1024,1024]{1,0:T(8,128)(2,1)} custom-call(bf16[2048,768]{1,0:T(8,128)(2,1)S(1)} %bitcast.150, bf16[2048,768]{1,0:T(8,128)(2,1)S(1)} %bitcast.153, bf16[1024,1536]{1,0:T(8,128)(2,1)S(1)} %copy-done.1, bf16[1024,1536]{1,0:T(8,128)(2,1)S(1)} %copy-done.1, bf16[4,32,1280]{2,1,0:T(8,128)(2,1)} %get-tuple-element.165.rest_0_, ...), custom_call_target="tpu_custom_call" | custom-call | flops 1450000000 | bytes 4600000 | tf_op jit(solution)/shard_map/input_back/pallas_call | solution.py:363
  402.6 5.5 %product.15 = bf16[1024,768]{1,0:T(8,128)(2,1)S(1)} custom-call(s32[4]{0:T(128)S(1)} %pad_add_fusion.1.where_ref, bf16[1024,1024]{1,0:T(8,128)(2,1)S(1)} %bitcast.172, bf16[1024,1024]{1,0:T(8,128)(2,1)} %collective-permute-done.theirs_ref.refs_1_, bf16[2048,768]{1,0:T(8,128)(2,1)S(1)} %bitcast.154, bf16[1024,1024]{1,0:T(8,128)(2,1)} %input_back.2.refs_3_), custom_call_target="tpu_custom_call" | custom-call | flops 1224155392 | bytes 3883527 | tf_op jit(solution)/shard_map/product/pallas_call | solution.py:806
  408.1 2.7 collective-permute-done.39.got_p
  417.0 2.2 collective-permute-done.38.refs_6_
  419.6 6.2 %update.3 = (f32[512,1024]{1,0:T(8,128)}, f32[512,1024]{1,0:T(8,128)}, f32[512,1024]{1,0:T(8,128)}, bf16[512,1024]{1,0:T(8,128)(2,1)}) custom-call(s32[4]{0:T(128)S(1)} %pad_add_fusion.1.where_ref, f32[512,1024]{1,0:T(8,128)S(1)} %copy-done.24, f32[512,1024]{1,0:T(8,128)S(1)} %copy-done.28, f32[512,1024]{1,0:T(8,128)S(1)} %copy-done.29, ...), custom_call_target="tpu_custom_call" | custom-call | flops 1450000000 | bytes 4600000 | tf_op jit(solution)/shard_map/update/pallas_call | solution.py:331
  427.4 6.8 %input_back.3.rest_0_ = f32[1024,1024]{1,0:T(8,128)} custom-call(bf16[2048,768]{1,0:T(8,128)(2,1)S(1)} %bitcast.151, bf16[2048,768]{1,0:T(8,128)(2,1)S(1)} %bitcast.155, bf16[1024,1536]{1,0:T(8,128)(2,1)S(1)} %copy-done.1, bf16[1024,1536]{1,0:T(8,128)(2,1)S(1)} %copy-done.1, bf16[1024,1024]{1,0:T(8,128)(2,1)S(1)} %copy-done.11, ...), custom_call_target="tpu_custom_call" | custom-call | flops 1450000000 | bytes 4600000 | tf_op jit(solution)/shard_map/input_back/pallas_call | solution.py:363
  434.2 2.2 copy-done.14
  438.1 2.7 collective-permute-start.46
  445.0 3.2 collective-permute-done.47.got_p
  449.9 3.1 collective-permute-done.46.rest_1_
  456.6 3.4 collective-permute-start.45
  459.9 6.9 %collective-permute-done.52.got = bf16[2,2,32,896]{3,2,1,0:T(8,128)(2,1)S(1)} collective-permute-done((bf16[2,2,32,896]{3,2,1,0:T(8,128)(2,1)S(1)}, bf16[2,2,32,896]{3,2,1,0:T(8,128)(2,1)S(1)}, u32[]{:S(2)}, u32[]{:S(2)}) %collective-permute-start.52) | collective-permute-done | bytes 229408 | tf_op jit(solution)/shard_map/ppermute | solution.py:139
  469.3 5.1 %update.4 = (f32[128,4096]{1,0:T(8,128)}, f32[128,4096]{1,0:T(8,128)}, f32[128,4096]{1,0:T(8,128)}, bf16[128,4096]{1,0:T(8,128)(2,1)}) custom-call(s32[4]{0:T(128)S(1)} %pad_add_fusion.1.where_ref, f32[128,4096]{1,0:T(8,128)S(1)} %copy-done.25, f32[128,4096]{1,0:T(8,128)S(1)} %copy-done.30, f32[128,4096]{1,0:T(8,128)S(1)} %copy-done.31, ...), custom_call_target="tpu_custom_call" | custom-call | flops 1450000000 | bytes 4600000 | tf_op jit(solution)/shard_map/update/pallas_call | solution.py:331
  482.7 6.4 %collective-permute-done.59.refs_10_ = bf16[2,32,896]{2,1,0:T(8,128)(2,1)S(1)} collective-permute-done((bf16[2,32,896]{2,1,0:T(8,128)(2,1)S(1)}, bf16[2,32,896]{2,1,0:T(8,128)(2,1)S(1)}, u32[]{:S(2)}, u32[]{:S(2)}) %collective-permute-start.59) | collective-permute-done | bytes 114720 | tf_op jit(solution)/shard_map/ppermute | solution.py:143
  493.1 5.4 %update.5 = (f32[4,128,1024]{2,1,0:T(8,128)}, f32[4,128,1024]{2,1,0:T(8,128)}, f32[4,128,1024]{2,1,0:T(8,128)}, bf16[4,128,1024]{2,1,0:T(8,128)(2,1)}) custom-call(s32[4]{0:T(128)S(1)} %pad_add_fusion.1.where_ref, f32[4,128,1024]{2,1,0:T(8,128)S(1)} %copy-done.21, f32[4,128,1024]{2,1,0:T(8,128)S(1)} %copy-done.32, f32[4,128,1024]{2,1,0:T(8,128)S(1)} %copy-done.33, ...), custom_call_target="tpu_custom_call" | custom-call | flops 1450000000 | bytes 4600000 | tf_op jit(solution)/shard_map/update/pallas_call | solution.py:331
  (336 shorter events, 116.0 us)
Async XLA Ops:
  2.8 11.0 %collective-permute-start.1 = (bf16[144,768]{1,0:T(8,128)(2,1)S(1)}, bf16[144,768]{1,0:T(8,128)(2,1)S(1)}, u32[]{:S(2)}, u32[]{:S(2)}) collective-permute-start(bf16[144,768]{1,0:T(8,128)(2,1)S(1)} %get-tuple-element.212), channel_id=1, source_target_pairs={{0,12},{2,14},{4,0},{6,2},{8,4},{10,6},{12,8},{14,10},{1,13},{3,15... | collective-permute-start | bytes 663560 | tf_op jit(solution)/shard_map/ppermute | solution.py:77
  7.9 18.9 %collective-permute-start.2 = (bf16[144,768]{1,0:T(8,128)(2,1)S(1)}, bf16[144,768]{1,0:T(8,128)(2,1)}, u32[]{:S(2)}, u32[]{:S(2)}) collective-permute-start(bf16[144,768]{1,0:T(8,128)(2,1)S(1)} %get-tuple-element.212), channel_id=1, source_target_pairs={{0,8},{2,10},{4,12},{6,14},{8,0},{10,2},{12,4},{14,6},{1,9},{3,11}... | collective-permute-start | bytes 663560 | tf_op jit(solution)/shard_map/ppermute | solution.py:77
  7.9 18.9 %collective-permute-start.3 = (bf16[144,768]{1,0:T(8,128)(2,1)S(1)}, bf16[144,768]{1,0:T(8,128)(2,1)S(1)}, u32[]{:S(2)}, u32[]{:S(2)}) collective-permute-start(bf16[144,768]{1,0:T(8,128)(2,1)S(1)} %get-tuple-element.212), channel_id=1, source_target_pairs={{0,4},{2,6},{4,8},{6,10},{8,12},{10,14},{12,0},{14,2},{1,5},{3,7},... | collective-permute-start | bytes 663560 | tf_op jit(solution)/shard_map/ppermute | solution.py:77
  8.9 60.9 %collective-permute-start = (bf16[1024,1024]{1,0:T(8,128)(2,1)S(1)}, bf16[1024,1024]{1,0:T(8,128)(2,1)}, u32[]{:S(2)}, u32[]{:S(2)}) collective-permute-start(bf16[1024,1024]{1,0:T(8,128)(2,1)S(1)} %bitcast.169), channel_id=1, source_target_pairs={{0,1},{1,0},{2,3},{3,2},{4,5},{5,4},{6,7},{7,6},{8,9},{9,8},{10,11... | collective-permute-start | bytes 6291464 | tf_op jit(solution)/shard_map/ppermute | solution.py:69
  28.6 20.7 %collective-permute-start.4 = (bf16[4,144,768]{2,1,0:T(8,128)(2,1)S(1)}, bf16[4,144,768]{2,1,0:T(8,128)(2,1)}, u32[]{:S(2)}, u32[]{:S(2)}) collective-permute-start(bf16[4,144,768]{2,1,0:T(8,128)(2,1)S(1)} %pad_maximum_fusion.rest_1_.rest_0_), channel_id=1, source_target_pairs={{0,2},{2,0},{4,6},{6,4},{8,10},{10,8},{12,14},{14,12},{1,3},{3,1},... | collective-permute-start | bytes 2654216 | tf_op jit(solution)/shard_map/ppermute | solution.py:85
  30.2 20.3 %collective-permute-start.5 = (bf16[4,144,768]{2,1,0:T(8,128)(2,1)S(1)}, bf16[4,144,768]{2,1,0:T(8,128)(2,1)}, u32[]{:S(2)}, u32[]{:S(2)}) collective-permute-start(bf16[4,144,768]{2,1,0:T(8,128)(2,1)S(1)} %pad_maximum_fusion.rest_1_.rest_0_), channel_id=1, source_target_pairs={{0,16},{16,0},{1,17},{17,1},{2,18},{18,2},{3,19},{19,3},{4,20},{20... | collective-permute-start | bytes 2654216 | tf_op jit(solution)/shard_map/ppermute | solution.py:90
  34.9 29.0 %collective-permute-start.8 = (bf16[304,1024]{1,0:T(8,128)(2,1)S(1)}, bf16[304,1024]{1,0:T(8,128)(2,1)S(1)}, u32[]{:S(2)}, u32[]{:S(2)}) collective-permute-start(bf16[304,1024]{1,0:T(8,128)(2,1)S(1)} %relay.2.own), channel_id=1, source_target_pairs={{0,8},{2,10},{4,12},{6,14},{8,0},{10,2},{12,4},{14,6},{1,9},{3,11}... | collective-permute-start | bytes 1867784 | tf_op jit(solution)/shard_map/ppermute | solution.py:139
  52.1 11.8 %collective-permute-start.6 = (bf16[2,144,768]{2,1,0:T(8,128)(2,1)S(1)}, bf16[2,144,768]{2,1,0:T(8,128)(2,1)S(1)}, u32[]{:S(2)}, u32[]{:S(2)}) collective-permute-start(bf16[2,144,768]{2,1,0:T(8,128)(2,1)S(1)} %get-tuple-element.111), channel_id=1, source_target_pairs={{0,2},{2,0},{4,6},{6,4},{8,10},{10,8},{12,14},{14,12},{1,3},{3,1},... | collective-permute-start | bytes 1327112 | tf_op jit(solution)/shard_map/ppermute | solution.py:85
  52.7 11.2 %collective-permute-start.7 = (bf16[2,144,768]{2,1,0:T(8,128)(2,1)S(1)}, bf16[2,144,768]{2,1,0:T(8,128)(2,1)S(1)}, u32[]{:S(2)}, u32[]{:S(2)}) collective-permute-start(bf16[2,144,768]{2,1,0:T(8,128)(2,1)S(1)} %get-tuple-element.112), channel_id=1, source_target_pairs={{0,16},{16,0},{1,17},{17,1},{2,18},{18,2},{3,19},{19,3},{4,20},{20... | collective-permute-start | bytes 1327112 | tf_op jit(solution)/shard_map/ppermute | solution.py:90
  65.5 29.5 %collective-permute-start.9 = (bf16[2,304,1024]{2,1,0:T(8,128)(2,1)}, bf16[2,304,1024]{2,1,0:T(8,128)(2,1)}, u32[]{:S(2)}, u32[]{:S(2)}) collective-permute-start(bf16[2,304,1024]{2,1,0:T(8,128)(2,1)} %pair.1.rest_5_.rest_0_), channel_id=1, source_target_pairs={{0,4},{2,6},{4,0},{6,2},{8,12},{10,14},{12,8},{14,10},{1,5},{3,7},... | collective-permute-start | bytes 3735560 | tf_op jit(solution)/shard_map/ppermute | solution.py:139
  67.0 50.7 %collective-permute-start.11 = (bf16[2,304,1024]{2,1,0:T(8,128)(2,1)}, bf16[2,304,1024]{2,1,0:T(8,128)(2,1)}, u32[]{:S(2)}, u32[]{:S(2)}) collective-permute-start(bf16[2,304,1024]{2,1,0:T(8,128)(2,1)} %pair.1.rest_5_.rest_0_), channel_id=1, source_target_pairs={{0,2},{2,0},{4,6},{6,4},{8,10},{10,8},{12,14},{14,12},{1,3},{3,1},... | collective-permute-start | bytes 3735560 | tf_op jit(solution)/shard_map/ppermute | solution.py:85
  68.3 49.5 %collective-permute-start.13 = (bf16[2,304,1024]{2,1,0:T(8,128)(2,1)}, bf16[2,304,1024]{2,1,0:T(8,128)(2,1)}, u32[]{:S(2)}, u32[]{:S(2)}) collective-permute-start(bf16[2,304,1024]{2,1,0:T(8,128)(2,1)} %pair.1.rest_5_.rest_0_), channel_id=1, source_target_pairs={{0,16},{16,0},{1,17},{17,1},{2,18},{18,2},{3,19},{19,3},{4,20},{20... | collective-permute-start | bytes 3735560 | tf_op jit(solution)/shard_map/ppermute | solution.py:90
  98.3 28.3 %collective-permute-start.12 = (bf16[2,304,1024]{2,1,0:T(8,128)(2,1)S(1)}, bf16[2,304,1024]{2,1,0:T(8,128)(2,1)S(1)}, u32[]{:S(2)}, u32[]{:S(2)}) collective-permute-start(bf16[2,304,1024]{2,1,0:T(8,128)(2,1)S(1)} %relay.3.rest_0_.rest_1_), channel_id=1, source_target_pairs={{0,2},{2,0},{4,6},{6,4},{8,10},{10,8},{12,14},{14,12},{1,3},{3,1},... | collective-permute-start | bytes 3735560 | tf_op jit(solution)/shard_map/ppermute | solution.py:85
  98.9 28.1 %collective-permute-start.14 = (bf16[2,304,1024]{2,1,0:T(8,128)(2,1)S(1)}, bf16[2,304,1024]{2,1,0:T(8,128)(2,1)}, u32[]{:S(2)}, u32[]{:S(2)}) collective-permute-start(bf16[2,304,1024]{2,1,0:T(8,128)(2,1)S(1)} %relay.3.rest_0_.rest_1_), channel_id=1, source_target_pairs={{0,16},{16,0},{1,17},{17,1},{2,18},{18,2},{3,19},{19,3},{4,20},{20... | collective-permute-start | bytes 3735560 | tf_op jit(solution)/shard_map/ppermute | solution.py:90
  133.1 38.2 %collective-permute-start.17 = (bf16[12,304,1024]{2,1,0:T(8,128)(2,1)}, bf16[12,304,1024]{2,1,0:T(8,128)(2,1)}, u32[]{:S(2)}, u32[]{:S(2)}) collective-permute-start(bf16[12,304,1024]{2,1,0:T(8,128)(2,1)} %get-tuple-element.120.more_0_), channel_id=1, source_target_pairs={{0,1},{1,0},{2,3},{3,2},{4,5},{5,4},{6,7},{7,6},{8,9},{9,8},{10,11... | collective-permute-start | bytes 22413320 | tf_op jit(solution)/shard_map/ppermute | solution.py:69
  133.1 29.8 %collective-permute-start.15 = (bf16[2,304,1024]{2,1,0:T(8,128)(2,1)S(1)}, bf16[2,304,1024]{2,1,0:T(8,128)(2,1)S(1)}, u32[]{:S(2)}, u32[]{:S(2)}) collective-permute-start(bf16[2,304,1024]{2,1,0:T(8,128)(2,1)S(1)} %get-tuple-element.121), channel_id=1, source_target_pairs={{0,2},{2,0},{4,6},{6,4},{8,10},{10,8},{12,14},{14,12},{1,3},{3,1},... | collective-permute-start | bytes 3735560 | tf_op jit(solution)/shard_map/ppermute | solution.py:85
  134.6 29.5 %collective-permute-start.16 = (bf16[2,304,1024]{2,1,0:T(8,128)(2,1)S(1)}, bf16[2,304,1024]{2,1,0:T(8,128)(2,1)S(1)}, u32[]{:S(2)}, u32[]{:S(2)}) collective-permute-start(bf16[2,304,1024]{2,1,0:T(8,128)(2,1)S(1)} %get-tuple-element.122), channel_id=1, source_target_pairs={{0,16},{16,0},{1,17},{17,1},{2,18},{18,2},{3,19},{19,3},{4,20},{20... | collective-permute-start | bytes 3735560 | tf_op jit(solution)/shard_map/ppermute | solution.py:90
  244.8 34.1 %collective-permute-start.21 = (bf16[4,2,128,512]{3,2,1,0:T(8,128)(2,1)S(1)}, bf16[4,2,128,512]{3,2,1,0:T(8,128)(2,1)S(1)}, u32[]{:S(2)}, u32[]{:S(2)}) collective-permute-start(bf16[4,2,128,512]{3,2,1,0:T(8,128)(2,1)S(1)} %get-tuple-element.132.after_ref), channel_id=1, source_target_pairs={{0,2},{2,0},{4,6},{6,4},{8,10},{10,8},{12,14},{14,12},{1,3},{3,1},... | collective-permute-start | bytes 3145736 | tf_op jit(solution)/shard_map/ppermute | solution.py:85
  245.4 33.5 %collective-permute-start.22 = (bf16[4,2,128,512]{3,2,1,0:T(8,128)(2,1)S(1)}, bf16[4,2,128,512]{3,2,1,0:T(8,128)(2,1)S(1)}, u32[]{:S(2)}, u32[]{:S(2)}) collective-permute-start(bf16[4,2,128,512]{3,2,1,0:T(8,128)(2,1)S(1)} %get-tuple-element.140), channel_id=1, source_target_pairs={{0,16},{16,0},{1,17},{17,1},{2,18},{18,2},{3,19},{19,3},{4,20},{20... | collective-permute-start | bytes 3145736 | tf_op jit(solution)/shard_map/ppermute | solution.py:90
  284.0 13.5 %collective-permute-start.23 = (bf16[4,128,512]{2,1,0:T(8,128)(2,1)S(1)}, bf16[4,128,512]{2,1,0:T(8,128)(2,1)S(1)}, u32[]{:S(2)}, u32[]{:S(2)}) collective-permute-start(bf16[4,128,512]{2,1,0:T(8,128)(2,1)S(1)} %get-tuple-element.141.refs_2_), channel_id=1, source_target_pairs={{0,16},{16,0},{1,17},{17,1},{2,18},{18,2},{3,19},{19,3},{4,20},{20... | collective-permute-start | bytes 1572872 | tf_op jit(solution)/shard_map/ppermute | solution.py:90
  285.8 13.1 %collective-permute-start.24 = (bf16[4,128,512]{2,1,0:T(8,128)(2,1)S(1)}, bf16[4,128,512]{2,1,0:T(8,128)(2,1)S(1)}, u32[]{:S(2)}, u32[]{:S(2)}) collective-permute-start(bf16[4,128,512]{2,1,0:T(8,128)(2,1)S(1)} %get-tuple-element.142.refs_3_), channel_id=1, source_target_pairs={{0,2},{2,0},{4,6},{6,4},{8,10},{10,8},{12,14},{14,12},{1,3},{3,1},... | collective-permute-start | bytes 1572872 | tf_op jit(solution)/shard_map/ppermute | solution.py:85
  307.0 15.0 %collective-permute-start.25 = (bf16[1024,2048]{1,0:T(8,128)(2,1)}, bf16[1024,2048]{1,0:T(8,128)(2,1)S(1)}, u32[]{:S(2)}, u32[]{:S(2)}) collective-permute-start(bf16[1024,2048]{1,0:T(8,128)(2,1)} %product.11.refs_3_), channel_id=1, source_target_pairs={{0,1},{1,0},{2,3},{3,2},{4,5},{5,4},{6,7},{7,6},{8,9},{9,8},{10,11... | collective-permute-start | bytes 12582920 | tf_op jit(solution)/shard_map/ppermute | solution.py:69
  307.0 14.3 %collective-permute-start.26 = (bf16[2,2,128,512]{3,2,1,0:T(8,128)(2,1)S(1)}, bf16[2,2,128,512]{3,2,1,0:T(8,128)(2,1)S(1)}, u32[]{:S(2)}, u32[]{:S(2)}) collective-permute-start(bf16[2,2,128,512]{3,2,1,0:T(8,128)(2,1)S(1)} %get-tuple-element.145.refs_2_), channel_id=1, source_target_pairs={{0,4},{2,6},{4,0},{6,2},{8,12},{10,14},{12,8},{14,10},{1,5},{3,7},... | collective-permute-start | bytes 1572872 | tf_op jit(solution)/shard_map/ppermute | solution.py:139
  307.4 18.7 %collective-permute-start.20 = (bf16[1024,512]{1,0:T(8,128)(2,1)S(1)}, bf16[1024,512]{1,0:T(8,128)(2,1)S(1)}, u32[]{:S(2)}, u32[]{:S(2)}) collective-permute-start(bf16[1024,512]{1,0:T(8,128)(2,1)S(1)} %get-tuple-element.134), channel_id=1, source_target_pairs={{0,1},{1,0},{2,3},{3,2},{4,5},{5,4},{6,7},{7,6},{8,9},{9,8},{10,11... | collective-permute-start | bytes 3145736 | tf_op jit(solution)/shard_map/ppermute | solution.py:69
  324.0 25.5 %collective-permute-start.29 = (bf16[4,2,32,2048]{3,2,1,0:T(8,128)(2,1)S(1)}, bf16[4,2,32,2048]{3,2,1,0:T(8,128)(2,1)S(1)}, u32[]{:S(2)}, u32[]{:S(2)}) collective-permute-start(bf16[4,2,32,2048]{3,2,1,0:T(8,128)(2,1)S(1)} %get-tuple-element.149.refs_8_), channel_id=1, source_target_pairs={{0,2},{2,0},{4,6},{6,4},{8,10},{10,8},{12,14},{14,12},{1,3},{3,1},... | collective-permute-start | bytes 3145736 | tf_op jit(solution)/shard_map/ppermute | solution.py:85
  325.6 24.5 %collective-permute-start.30 = (bf16[4,2,32,2048]{3,2,1,0:T(8,128)(2,1)S(1)}, bf16[4,2,32,2048]{3,2,1,0:T(8,128)(2,1)S(1)}, u32[]{:S(2)}, u32[]{:S(2)}) collective-permute-start(bf16[4,2,32,2048]{3,2,1,0:T(8,128)(2,1)S(1)} %get-tuple-element.150.refs_9_), channel_id=1, source_target_pairs={{0,16},{16,0},{1,17},{17,1},{2,18},{18,2},{3,19},{19,3},{4,20},{20... | collective-permute-start | bytes 3145736 | tf_op jit(solution)/shard_map/ppermute | solution.py:90
  326.1 26.8 %collective-permute-start.28 = (bf16[1024,512]{1,0:T(8,128)(2,1)S(1)}, bf16[1024,512]{1,0:T(8,128)(2,1)S(1)}, u32[]{:S(2)}, u32[]{:S(2)}) collective-permute-start(bf16[1024,512]{1,0:T(8,128)(2,1)S(1)} %product.12.refs_3_), channel_id=1, source_target_pairs={{0,1},{1,0},{2,3},{3,2},{4,5},{5,4},{6,7},{7,6},{8,9},{9,8},{10,11... | collective-permute-start | bytes 3145736 | tf_op jit(solution)/shard_map/ppermute | solution.py:69
  326.1 15.2 %collective-permute-start.27 = (bf16[2,128,512]{2,1,0:T(8,128)(2,1)S(1)}, bf16[2,128,512]{2,1,0:T(8,128)(2,1)S(1)}, u32[]{:S(2)}, u32[]{:S(2)}) collective-permute-start(bf16[2,128,512]{2,1,0:T(8,128)(2,1)S(1)} %get-tuple-element.148.refs_8_), channel_id=1, source_target_pairs={{0,8},{2,10},{4,12},{6,14},{8,0},{10,2},{12,4},{14,6},{1,9},{3,11}... | collective-permute-start | bytes 786440 | tf_op jit(solution)/shard_map/ppermute | solution.py:139
  357.0 29.7 %collective-permute-start.31 = (bf16[4,2,32,1280]{3,2,1,0:T(8,128)(2,1)}, bf16[4,2,32,1280]{3,2,1,0:T(8,128)(2,1)}, u32[]{:S(2)}, u32[]{:S(2)}) collective-permute-start(bf16[4,2,32,1280]{3,2,1,0:T(8,128)(2,1)} %get-tuple-element.157.refs_8_), channel_id=1, source_target_pairs={{0,2},{2,0},{4,6},{6,4},{8,10},{10,8},{12,14},{14,12},{1,3},{3,1},... | collective-permute-start | bytes 1966088 | tf_op jit(solution)/shard_map/ppermute | solution.py:85
  357.5 29.2 %collective-permute-start.32 = (bf16[4,2,32,1280]{3,2,1,0:T(8,128)(2,1)}, bf16[4,2,32,1280]{3,2,1,0:T(8,128)(2,1)}, u32[]{:S(2)}, u32[]{:S(2)}) collective-permute-start(bf16[4,2,32,1280]{3,2,1,0:T(8,128)(2,1)} %get-tuple-element.158.refs_9_), channel_id=1, source_target_pairs={{0,16},{16,0},{1,17},{17,1},{2,18},{18,2},{3,19},{19,3},{4,20},{20... | collective-permute-start | bytes 1966088 | tf_op jit(solution)/shard_map/ppermute | solution.py:90
  358.5 26.6 %collective-permute-start.33 = (bf16[4,32,2048]{2,1,0:T(8,128)(2,1)}, bf16[4,32,2048]{2,1,0:T(8,128)(2,1)S(1)}, u32[]{:S(2)}, u32[]{:S(2)}) collective-permute-start(bf16[4,32,2048]{2,1,0:T(8,128)(2,1)} %get-tuple-element.155.refs_12_), channel_id=1, source_target_pairs={{0,16},{16,0},{1,17},{17,1},{2,18},{18,2},{3,19},{19,3},{4,20},{20... | collective-permute-start | bytes 1572872 | tf_op jit(solution)/shard_map/ppermute | solution.py:90
  359.6 25.6 %collective-permute-start.34 = (bf16[4,32,2048]{2,1,0:T(8,128)(2,1)}, bf16[4,32,2048]{2,1,0:T(8,128)(2,1)S(1)}, u32[]{:S(2)}, u32[]{:S(2)}) collective-permute-start(bf16[4,32,2048]{2,1,0:T(8,128)(2,1)} %get-tuple-element.156.refs_13_), channel_id=1, source_target_pairs={{0,2},{2,0},{4,6},{6,4},{8,10},{10,8},{12,14},{14,12},{1,3},{3,1},... | collective-permute-start | bytes 1572872 | tf_op jit(solution)/shard_map/ppermute | solution.py:85
  394.8 31.0 %collective-permute-start.35 = (bf16[1024,1024]{1,0:T(8,128)(2,1)}, bf16[1024,1024]{1,0:T(8,128)(2,1)}, u32[]{:S(2)}, u32[]{:S(2)}) collective-permute-start(bf16[1024,1024]{1,0:T(8,128)(2,1)} %input_back.2.refs_3_), channel_id=1, source_target_pairs={{0,1},{1,0},{2,3},{3,2},{4,5},{5,4},{6,7},{7,6},{8,9},{9,8},{10,11... | collective-permute-start | bytes 6291464 | tf_op jit(solution)/shard_map/ppermute | solution.py:69
  394.9 19.6 %collective-permute-start.36 = (bf16[2,128,512]{2,1,0:T(8,128)(2,1)S(1)}, bf16[2,128,512]{2,1,0:T(8,128)(2,1)}, u32[]{:S(2)}, u32[]{:S(2)}) collective-permute-start(bf16[2,128,512]{2,1,0:T(8,128)(2,1)S(1)} %fold_line.4.refs_3_), channel_id=1, source_target_pairs={{0,16},{16,0},{1,17},{17,1},{2,18},{18,2},{3,19},{19,3},{4,20},{20... | collective-permute-start | bytes 786440 | tf_op jit(solution)/shard_map/ppermute | solution.py:90
  396.6 19.6 %collective-permute-start.37 = (bf16[2,128,512]{2,1,0:T(8,128)(2,1)S(1)}, bf16[2,128,512]{2,1,0:T(8,128)(2,1)}, u32[]{:S(2)}, u32[]{:S(2)}) collective-permute-start(bf16[2,128,512]{2,1,0:T(8,128)(2,1)S(1)} %fold_line.4.refs_3_), channel_id=1, source_target_pairs={{0,1},{1,0},{2,3},{3,2},{4,5},{5,4},{6,7},{7,6},{8,9},{9,8},{10,11... | collective-permute-start | bytes 786440 | tf_op jit(solution)/shard_map/ppermute | solution.py:69
  396.9 13.9 %collective-permute-start.39 = (bf16[4,32,1280]{2,1,0:T(8,128)(2,1)}, bf16[4,32,1280]{2,1,0:T(8,128)(2,1)}, u32[]{:S(2)}, u32[]{:S(2)}) collective-permute-start(bf16[4,32,1280]{2,1,0:T(8,128)(2,1)} %get-tuple-element.165.rest_0_), channel_id=1, source_target_pairs={{0,16},{16,0},{1,17},{17,1},{2,18},{18,2},{3,19},{19,3},{4,20},{20... | collective-permute-start | bytes 983048 | tf_op jit(solution)/shard_map/ppermute | solution.py:90
  397.3 14.5 %collective-permute-start.40 = (bf16[4,32,1280]{2,1,0:T(8,128)(2,1)}, bf16[4,32,1280]{2,1,0:T(8,128)(2,1)}, u32[]{:S(2)}, u32[]{:S(2)}) collective-permute-start(bf16[4,32,1280]{2,1,0:T(8,128)(2,1)} %get-tuple-element.166.rest_1_), channel_id=1, source_target_pairs={{0,2},{2,0},{4,6},{6,4},{8,10},{10,8},{12,14},{14,12},{1,3},{3,1},... | collective-permute-start | bytes 983048 | tf_op jit(solution)/shard_map/ppermute | solution.py:85
  411.8 25.4 %collective-permute-start.42 = (bf16[2,2,32,2048]{3,2,1,0:T(8,128)(2,1)S(1)}, bf16[2,2,32,2048]{3,2,1,0:T(8,128)(2,1)S(1)}, u32[]{:S(2)}, u32[]{:S(2)}) collective-permute-start(bf16[2,2,32,2048]{3,2,1,0:T(8,128)(2,1)S(1)} %copy-done.44), channel_id=1, source_target_pairs={{0,4},{2,6},{4,0},{6,2},{8,12},{10,14},{12,8},{14,10},{1,5},{3,7},... | collective-permute-start | bytes 1572872 | tf_op jit(solution)/shard_map/ppermute | solution.py:139
  414.5 19.7 %collective-permute-start.43 = (bf16[4,2,32,896]{3,2,1,0:T(8,128)(2,1)S(1)}, bf16[4,2,32,896]{3,2,1,0:T(8,128)(2,1)S(1)}, u32[]{:S(2)}, u32[]{:S(2)}) collective-permute-start(bf16[4,2,32,896]{3,2,1,0:T(8,128)(2,1)S(1)} %get-tuple-element.174.refs_7_), channel_id=1, source_target_pairs={{0,2},{2,0},{4,6},{6,4},{8,10},{10,8},{12,14},{14,12},{1,3},{3,1},... | collective-permute-start | bytes 1376264 | tf_op jit(solution)/shard_map/ppermute | solution.py:85
  416.2 17.9 %collective-permute-start.44 = (bf16[4,2,32,896]{3,2,1,0:T(8,128)(2,1)S(1)}, bf16[4,2,32,896]{3,2,1,0:T(8,128)(2,1)S(1)}, u32[]{:S(2)}, u32[]{:S(2)}) collective-permute-start(bf16[4,2,32,896]{3,2,1,0:T(8,128)(2,1)S(1)} %get-tuple-element.175.refs_8_), channel_id=1, source_target_pairs={{0,16},{16,0},{1,17},{17,1},{2,18},{18,2},{3,19},{19,3},{4,20},{20... | collective-permute-start | bytes 1376264 | tf_op jit(solution)/shard_map/ppermute | solution.py:90
  419.2 25.2 %collective-permute-start.41 = (bf16[2,2,32,1280]{3,2,1,0:T(8,128)(2,1)S(1)}, bf16[2,2,32,1280]{3,2,1,0:T(8,128)(2,1)S(1)}, u32[]{:S(2)}, u32[]{:S(2)}) collective-permute-start(bf16[2,2,32,1280]{3,2,1,0:T(8,128)(2,1)S(1)} %get-tuple-element.173.refs_8_), channel_id=1, source_target_pairs={{0,4},{2,6},{4,0},{6,2},{8,12},{10,14},{12,8},{14,10},{1,5},{3,7},... | collective-permute-start | bytes 983048 | tf_op jit(solution)/shard_map/ppermute | solution.py:139
  438.1 14.9 %collective-permute-start.46 = (bf16[2,32,2048]{2,1,0:T(8,128)(2,1)S(1)}, bf16[2,32,2048]{2,1,0:T(8,128)(2,1)S(1)}, u32[]{:S(2)}, u32[]{:S(2)}) collective-permute-start(bf16[2,32,2048]{2,1,0:T(8,128)(2,1)S(1)} %get-tuple-element.183.rest_0_), channel_id=1, source_target_pairs={{0,8},{2,10},{4,12},{6,14},{8,0},{10,2},{12,4},{14,6},{1,9},{3,11}... | collective-permute-start | bytes 786440 | tf_op jit(solution)/shard_map/ppermute | solution.py:139
  453.6 15.6 %collective-permute-start.49 = (bf16[2,32,2048]{2,1,0:T(8,128)(2,1)S(1)}, bf16[2,32,2048]{2,1,0:T(8,128)(2,1)S(1)}, u32[]{:S(2)}, u32[]{:S(2)}) collective-permute-start(bf16[2,32,2048]{2,1,0:T(8,128)(2,1)S(1)} %fold_line.5.rest_0_.refs_3_), channel_id=1, source_target_pairs={{0,16},{16,0},{1,17},{17,1},{2,18},{18,2},{3,19},{19,3},{4,20},{20... | collective-permute-start | bytes 786440 | tf_op jit(solution)/shard_map/ppermute | solution.py:90
  455.0 14.1 %collective-permute-start.50 = (bf16[2,32,2048]{2,1,0:T(8,128)(2,1)S(1)}, bf16[2,32,2048]{2,1,0:T(8,128)(2,1)S(1)}, u32[]{:S(2)}, u32[]{:S(2)}) collective-permute-start(bf16[2,32,2048]{2,1,0:T(8,128)(2,1)S(1)} %fold_line.5.rest_0_.refs_3_), channel_id=1, source_target_pairs={{0,1},{1,0},{2,3},{3,2},{4,5},{5,4},{6,7},{7,6},{8,9},{9,8},{10,11... | collective-permute-start | bytes 786440 | tf_op jit(solution)/shard_map/ppermute | solution.py:69
  455.1 14.1 %collective-permute-start.51 = (bf16[2,32,2048]{2,1,0:T(8,128)(2,1)S(1)}, bf16[2,32,2048]{2,1,0:T(8,128)(2,1)S(1)}, u32[]{:S(2)}, u32[]{:S(2)}) collective-permute-start(bf16[2,32,2048]{2,1,0:T(8,128)(2,1)S(1)} %fold_line.5.rest_0_.refs_3_), channel_id=1, source_target_pairs={{0,17},{1,16},{16,1},{17,0},{2,19},{3,18},{18,3},{19,2},{4,21},{5,... | collective-permute-start | bytes 786440 | tf_op jit(solution)/shard_map/ppermute | solution.py:143
  455.8 11.0 %collective-permute-start.52 = (bf16[2,2,32,896]{3,2,1,0:T(8,128)(2,1)S(1)}, bf16[2,2,32,896]{3,2,1,0:T(8,128)(2,1)S(1)}, u32[]{:S(2)}, u32[]{:S(2)}) collective-permute-start(bf16[2,2,32,896]{3,2,1,0:T(8,128)(2,1)S(1)} %get-tuple-element.189.rest_2_), channel_id=1, source_target_pairs={{0,4},{2,6},{4,0},{6,2},{8,12},{10,14},{12,8},{14,10},{1,5},{3,7},... | collective-permute-start | bytes 688136 | tf_op jit(solution)/shard_map/ppermute | solution.py:139
  456.6 17.8 %collective-permute-start.45 = (bf16[2,32,1280]{2,1,0:T(8,128)(2,1)S(1)}, bf16[2,32,1280]{2,1,0:T(8,128)(2,1)S(1)}, u32[]{:S(2)}, u32[]{:S(2)}) collective-permute-start(bf16[2,32,1280]{2,1,0:T(8,128)(2,1)S(1)} %get-tuple-element.185.rest_0_), channel_id=1, source_target_pairs={{0,8},{2,10},{4,12},{6,14},{8,0},{10,2},{12,4},{14,6},{1,9},{3,11}... | collective-permute-start | bytes 491528 | tf_op jit(solution)/shard_map/ppermute | solution.py:139
  478.7 11.1 %collective-permute-start.53 = (bf16[2,32,1280]{2,1,0:T(8,128)(2,1)S(1)}, bf16[2,32,1280]{2,1,0:T(8,128)(2,1)S(1)}, u32[]{:S(2)}, u32[]{:S(2)}) collective-permute-start(bf16[2,32,1280]{2,1,0:T(8,128)(2,1)S(1)} %fold_line.6.rest_2_.refs_3_), channel_id=1, source_target_pairs={{0,16},{16,0},{1,17},{17,1},{2,18},{18,2},{3,19},{19,3},{4,20},{20... | collective-permute-start | bytes 491528 | tf_op jit(solution)/shard_map/ppermute | solution.py:90
  (89 other events, 657.1 us)
where the time goes:
time: 508 us; the launch traced here: 499 us
  Pallas kernels  259 us (51%)
  waiting for transfers between devices  126 us (25%)
  starting transfers between devices  58.1 us (11%)
  local copies, waits for them, and re-layouts  50.3 us (10%)
    pallas_call x2, Pallas kernels, ffn_call(): pl.pallas_call(kernel, grid=(steps,), in_specs=[pl.BlockSpec(memory_space...  82.8 us
    pallas_call x4, Pallas kernels, attention_call(): pl.pallas_call(kernel, grid=(seqs, pairs), in_specs=[spec(a, first) for a...  57.9 us
    pallas_call x8, Pallas kernels, product(): pl.pallas_call(functools.partial(product_kernel, len(lefts), stacked, len...  43 us
    unnamed x166, local copies, waits for them, and re-layouts  42.4 us
    ppermute x10, waiting for transfers between devices, swap_outer(): return lax.ppermute(value, 'shard', pairs)  41.2 us
    ppermute x13, waiting for transfers between devices, shift_inner(): return lax.ppermute(value, 'shard', pairs)  36.9 us
    pallas_call x22, Pallas kernels, small_call(): pl.pallas_call(functools.partial(kernel, len(ins), len(after)), in_specs=...  26.6 us
    ppermute x17, waiting for transfers between devices, shift_replica(): lax.ppermute(value, 'replica', [(r, (r + step) % size) for r in range(siz...  18.5 us
  transfers between devices with their start and end apart: 60, of which 25 were waited for; matrix products, arithmetic and copies ran while one was open for 2% of the time, Pallas kernels for 33%

commit v1 on v0

--- a/solution.py
+++ b/solution.py
@@ -1239,8 +1239,8 @@
     attn_states = (attn_master, attn_moment, attn_square)
     if square:
         inner = Sum(where, inner_chips)
-        done = outer.turn((out_kept,))
-        done = inner.merge(done)
+        done = inner.merge((out_kept,))
+        done = outer.turn(done)
         grad_a, sums_a = back(0, done)
         done = outer.line((grad_a,))
         ours = by_shard(product(where, [rows, rows_theirs], grad_a, None, done))

time: 508 us -> 503 us (level)
    ppermute x10, waiting for transfers between devices: 41.2 us -> 33.9 us  [swap_outer(): return lax.ppermute(value, 'shard', pairs)]
  transfers between devices with their start and end apart: 60 -> 60, of which waited for: 25 -> 25; matrix products, arithmetic and copies ran while one was open for 2% -> 2% of each run, Pallas kernels for 33% -> 34%
where the time goes in v1:
time: 503 us; the launch traced here: 494 us
  Pallas kernels  258 us (51%)
  waiting for transfers between devices  125 us (25%)
  starting transfers between devices  54 us (11%)
  local copies, waits for them, and re-layouts  50.2 us (10%)
    pallas_call x2, Pallas kernels, ffn_call(): pl.pallas_call(kernel, grid=(steps,), in_specs=[pl.BlockSpec(memory_space...  82.8 us
    pallas_call x4, Pallas kernels, attention_call(): pl.pallas_call(kernel, grid=(seqs, pairs), in_specs=[spec(a, first) for a...  57.9 us
    pallas_call x8, Pallas kernels, product(): pl.pallas_call(functools.partial(product_kernel, len(lefts), stacked, len...  43 us
    unnamed x166, local copies, waits for them, and re-layouts  42.4 us
    ppermute x13, waiting for transfers between devices, shift_inner(): return lax.ppermute(value, 'shard', pairs)  36.4 us
    ppermute x10, waiting for transfers between devices, swap_outer(): return lax.ppermute(value, 'shard', pairs)  33.9 us
    pallas_call x22, Pallas kernels, small_call(): pl.pallas_call(functools.partial(kernel, len(ins), len(after)), in_specs=...  26.5 us
    ppermute x17, waiting for transfers between devices, shift_replica(): lax.ppermute(value, 'replica', [(r, (r + step) % size) for r in range(siz...  21.1 us
  transfers between devices with their start and end apart: 60, of which 25 were waited for; matrix products, arithmetic and copies ran while one was open for 2% of the time, Pallas kernels for 34%

profile of v1, /device:TPU:0, one launch (start us, length us, event | category | flops | bytes accessed | tf_op | source)
XLA Modules:
  0.0 493.9 jit_solution(9644170326727300355)
XLA Ops:
  2.8 5.1 %collective-permute-start.1 = (bf16[144,768]{1,0:T(8,128)(2,1)S(1)}, bf16[144,768]{1,0:T(8,128)(2,1)S(1)}, u32[]{:S(2)}, u32[]{:S(2)}) collective-permute-start(bf16[144,768]{1,0:T(8,128)(2,1)S(1)} %get-tuple-element.212), channel_id=1, source_target_pairs={{0,12},{2,14},{4,0},{6,2},{8,4},{10,6},{12,8},{14,10},{1,13},{3,15... | collective-permute-start | bytes 663560 | tf_op jit(solution)/shard_map/ppermute | solution.py:77
  8.9 4.9 collective-permute-done.1
  13.8 13.0 %collective-permute-done.2 = bf16[144,768]{1,0:T(8,128)(2,1)} collective-permute-done((bf16[144,768]{1,0:T(8,128)(2,1)S(1)}, bf16[144,768]{1,0:T(8,128)(2,1)}, u32[]{:S(2)}, u32[]{:S(2)}) %collective-permute-start.2) | collective-permute-done | bytes 221216 | tf_op jit(solution)/shard_map/ppermute | solution.py:77
  34.9 2.8 collective-permute-start.8
  37.6 11.7 %collective-permute-done.4.near_x.rest_1_ = bf16[4,144,768]{2,1,0:T(8,128)(2,1)} collective-permute-done((bf16[4,144,768]{2,1,0:T(8,128)(2,1)S(1)}, bf16[4,144,768]{2,1,0:T(8,128)(2,1)}, u32[]{:S(2)}, u32[]{:S(2)}) %collective-permute-start.4) | collective-permute-done | bytes 884768 | tf_op jit(solution)/shard_map/ppermute | solution.py:85
  54.2 9.7 %collective-permute-done.8.other = bf16[304,1024]{1,0:T(8,128)(2,1)S(1)} collective-permute-done((bf16[304,1024]{1,0:T(8,128)(2,1)S(1)}, bf16[304,1024]{1,0:T(8,128)(2,1)S(1)}, u32[]{:S(2)}, u32[]{:S(2)}) %collective-permute-start.8) | collective-permute-done | bytes 622624 | tf_op jit(solution)/shard_map/ppermute | solution.py:139
  70.8 12.0 %project.1 = (bf16[2048,1536]{1,0:T(8,128)(2,1)}, bf16[1024,1536]{1,0:T(8,128)(2,1)}) custom-call(s32[16]{0:T(128)S(1)} %stack.90.row_ref, s32[16]{0:T(128)S(1)} %stack.93.column_ref, bf16[1024,1024]{1,0:T(8,128)(2,1)S(1)} %bitcast.170, bf16[1024,1024]{1,0:T(8,128)(2,1)} %collective-permute-done.theirs_ref.refs_1_, f32[1,1536]{1,0:T(1,128)S(1)} %reshape.159.bias_ref, ...), custom_call_target="tpu_custom_call" | custom-call | flops 3190000128 | bytes 10120000 | tf_op jit(solution)/shard_map/project/pallas_call | solution.py:451
  82.8 12.2 %collective-permute-done.9.rest_0_ = bf16[2,304,1024]{2,1,0:T(8,128)(2,1)} collective-permute-done((bf16[2,304,1024]{2,1,0:T(8,128)(2,1)}, bf16[2,304,1024]{2,1,0:T(8,128)(2,1)}, u32[]{:S(2)}, u32[]{:S(2)}) %collective-permute-start.9) | collective-permute-done | bytes 1245216 | tf_op jit(solution)/shard_map/ppermute | solution.py:139
  101.1 2.8 copy-done.58
  103.9 13.9 %attend.2 = (bf16[4,256,512]{2,1,0:T(8,128)(2,1)S(1)}, bf16[4,256,512]{2,1,0:T(8,128)(2,1)}, f32[4,8,512]{2,1,0:T(8,128)S(1)}) custom-call(s32[4,1,512]{2,1,0:T(1,128)S(1)} %broadcast_in_dim.9.seg_row_ref.refs_0_, s32[4,512,1]{2,1,0:T(8,128)S(1)} %copy.63.seg_col_ref.refs_1_, bf16[2,4,256,1536]{3,2,1,0:T(8,128)(2,1)S(1)} %bitcast.181, ...), custom_call_target="tpu_custom_call" | custom-call | flops 3769999872 | bytes 11960000 | tf_op jit(solution)/shard_map/attend/pallas_call | solution.py:986
  117.8 8.8 %collective-permute-done.12.rest_3_ = bf16[2,304,1024]{2,1,0:T(8,128)(2,1)S(1)} collective-permute-done((bf16[2,304,1024]{2,1,0:T(8,128)(2,1)S(1)}, bf16[2,304,1024]{2,1,0:T(8,128)(2,1)S(1)}, u32[]{:S(2)}, u32[]{:S(2)}) %collective-permute-start.12) | collective-permute-done | bytes 1245216 | tf_op jit(solution)/shard_map/ppermute | solution.py:85
  127.0 6.1 %bulk.2 = (bf16[12,304,1024]{2,1,0:T(8,128)(2,1)}, bf16[2,304,1024]{2,1,0:T(8,128)(2,1)S(1)}, bf16[2,304,1024]{2,1,0:T(8,128)(2,1)S(1)}) custom-call(s32[4]{0:T(128)S(1)} %pad_add_fusion.1.where_ref, bf16[2,304,1024]{2,1,0:T(8,128)(2,1)} %pair.1.rest_5_.rest_0_, bf16[2,304,1024]{2,1,0:T(8,128)(2,1)S(1)} %relay.3.rest_0_.rest_1_, ...), custom_call_target="tpu_custom_call" | custom-call | flops 290000000 | bytes 920000 | tf_op jit(solution)/shard_map/bulk/pallas_call | solution.py:160
  135.1 13.9 %attend.3 = (bf16[4,256,512]{2,1,0:T(8,128)(2,1)S(1)}, bf16[4,256,512]{2,1,0:T(8,128)(2,1)}, f32[4,8,512]{2,1,0:T(8,128)S(1)}) custom-call(s32[4,1,512]{2,1,0:T(1,128)S(1)} %broadcast_in_dim.9.seg_row_ref.refs_0_, s32[4,512,1]{2,1,0:T(8,128)S(1)} %copy.63.seg_col_ref.refs_1_, ...), custom_call_target="tpu_custom_call", output_to_operand_aliasing={{0}: (3, {}), {1}: (4, {}), {2}: (5, {})} | custom-call | flops 3769999872 | bytes 11960000 | tf_op jit(solution)/shard_map/attend/pallas_call | solution.py:986
  149.0 13.9 %collective-permute-done.15.rest_0_ = bf16[2,304,1024]{2,1,0:T(8,128)(2,1)S(1)} collective-permute-done((bf16[2,304,1024]{2,1,0:T(8,128)(2,1)S(1)}, bf16[2,304,1024]{2,1,0:T(8,128)(2,1)S(1)}, u32[]{:S(2)}, u32[]{:S(2)}) %collective-permute-start.15) | collective-permute-done | bytes 1245216 | tf_op jit(solution)/shard_map/ppermute | solution.py:85
  168.5 2.4 collective-permute-done.10.theirs_ref.refs_1_
  171.9 50.7 %ffn.1 = (bf16[1024,4096]{1,0:T(8,128)(2,1)}, bf16[1024,4096]{1,0:T(8,128)(2,1)}, bf16[1024,4096]{1,0:T(8,128)(2,1)}, bf16[4096,1024]{1,0:T(8,128)(2,1)}, bf16[1...) custom-call(s32[1]{0:T(128)} %bitcast.core_ref, ...), custom_call_target="tpu_custom_call" | custom-call | flops 11600000000 | bytes 36800000 | tf_op jit(solution)/shard_map/ffn/pallas_call | solution.py:730
  222.6 3.4 copy-done.9
  227.6 7.3 %product.8.refs_2_ = bf16[4096,512]{1,0:T(8,128)(2,1)S(1)} custom-call(s32[4]{0:T(128)S(1)} %pad_add_fusion.1.where_ref, bf16[1024,4096]{1,0:T(8,128)(2,1)S(1)} %copy-done.9, bf16[1024,1024]{1,0:T(8,128)(2,1)S(1)} %copy-done.19), custom_call_target="tpu_custom_call" | custom-call | flops 1535540480 | bytes 4871369 | tf_op jit(solution)/shard_map/product/pallas_call | solution.py:806
  235.3 7.3 %product.9 = bf16[4096,512]{1,0:T(8,128)(2,1)S(1)} custom-call(s32[4]{0:T(128)S(1)} %pad_add_fusion.1.where_ref, bf16[1024,4096]{1,0:T(8,128)(2,1)S(1)} %copy-done.9, bf16[1024,1024]{1,0:T(8,128)(2,1)S(1)} %copy-done.19, bf16[4096,512]{1,0:T(8,128)(2,1)S(1)} %product.8.refs_2_), custom_call_target="tpu_custom_call" | custom-call | flops 1535540480 | bytes 4871369 | tf_op jit(solution)/shard_map/product/pallas_call | solution.py:806
  245.7 32.2 %ffn_back.1 = (bf16[1024,4096]{1,0:T(8,128)(2,1)}, bf16[1024,1024]{1,0:T(8,128)(2,1)S(1)}, bf16[1024,512]{1,0:T(8,128)(2,1)S(1)}, bf16[1024,512]{1,0:T(8,128)(2,1)S(1)}, f32[8,1024]{1,0:T(8,128)S(1)}) custom-call(s32[1]{0:T(128)} %bitcast.core_ref, bf16[1024,1024]{1,0:T(8,128)(2,1)S(1)} %copy-done.20, bf16[1024,4096]{1,0:T(8,128)(2,1)} %get-tuple-element.125.slope_ref, ...), custom_call_target="tpu_custom_call" | custom-call | flops 11600000000 | bytes 36800000 | tf_op jit(solution)/shard_map/ffn_back/pallas_call | solution.py:730
  278.9 4.1 copy-done.2
  287.3 5.7 %product.10.rest_0_ = bf16[1024,2048]{1,0:T(8,128)(2,1)S(1)} custom-call(s32[4]{0:T(128)S(1)} %pad_add_fusion.1.where_ref, bf16[1024,1024]{1,0:T(8,128)(2,1)S(1)} %copy-done.15, bf16[1024,4096]{1,0:T(8,128)(2,1)S(1)} %copy-done.3, bf16[4,128,512]{2,1,0:T(8,128)(2,1)S(1)} %get-tuple-element.141.refs_2_, bf16[4,128,512]{2,1,0:T(8,128)(2,1)S(1)} %get-tuple-element.143.refs_3_), custom_call_target="tpu_custom_call" | custom-call | flops 1535540480 | bytes 4871369 | tf_op jit(solution)/shard_map/product/pallas_call | solution.py:806
  293.0 4.5 collective-permute-done.23.got_p
  299.7 7.3 %product.11.refs_3_ = bf16[1024,2048]{1,0:T(8,128)(2,1)} custom-call(s32[4]{0:T(128)S(1)} %pad_add_fusion.1.where_ref, bf16[1024,1024]{1,0:T(8,128)(2,1)S(1)} %copy-done.15, bf16[1024,4096]{1,0:T(8,128)(2,1)S(1)} %copy-done.3, bf16[2,2,128,512]{3,2,1,0:T(8,128)(2,1)S(1)} %get-tuple-element.146.refs_2_), custom_call_target="tpu_custom_call" | custom-call | flops 1535540480 | bytes 4871369 | tf_op jit(solution)/shard_map/product/pallas_call | solution.py:806
  312.2 3.6 collective-permute-done.26
  322.1 15.1 %attend_back.2 = (bf16[2,4,256,768]{3,2,1,0:T(8,128)(2,1)S(1)}, f32[8,256]{1,0:T(8,128)S(1)}) custom-call(s32[4,1,512]{2,1,0:T(1,128)S(1)} %broadcast_in_dim.9.seg_row_ref.refs_0_, s32[4,512,1]{2,1,0:T(8,128)S(1)} %copy-done.36, bf16[2,4,256,1536]{3,2,1,0:T(8,128)(2,1)S(1)} %bitcast.185, bf16[4,256,512]{2,1,0:T(8,128)(2,1)S(1)} %copy-done.13, ...), custom_call_target="tpu_custom_call" | custom-call | flops 4292000000 | bytes 13616000 | tf_op jit(solution)/shard_map/attend_back/pallas_call | solution.py:986
  340.0 5.5 %product.14 = bf16[1024,768]{1,0:T(8,128)(2,1)S(1)} custom-call(s32[4]{0:T(128)S(1)} %pad_add_fusion.1.where_ref, bf16[1024,1024]{1,0:T(8,128)(2,1)S(1)} %bitcast.171, bf16[1024,1024]{1,0:T(8,128)(2,1)} %collective-permute-done.theirs_ref.refs_1_, bf16[2048,768]{1,0:T(8,128)(2,1)S(1)} %bitcast.149, bf16[2,128,512]{2,1,0:T(8,128)(2,1)S(1)} %fold_line.4.refs_3_), custom_call_target="tpu_custom_call" | custom-call | flops 1224155392 | bytes 3883527 | tf_op jit(solution)/shard_map/product/pallas_call | solution.py:806
  347.3 2.5 merge.6
  357.5 2.8 copy-done.60
  361.5 15.1 %attend_back.3 = (bf16[2,4,256,768]{3,2,1,0:T(8,128)(2,1)S(1)}, f32[8,256]{1,0:T(8,128)S(1)}) custom-call(s32[4,1,512]{2,1,0:T(1,128)S(1)} %broadcast_in_dim.9.seg_row_ref.refs_0_, s32[4,512,1]{2,1,0:T(8,128)S(1)} %copy-done.36, bf16[2,4,256,1536]{3,2,1,0:T(8,128)(2,1)S(1)} %bitcast.186, bf16[4,256,512]{2,1,0:T(8,128)(2,1)S(1)} %copy-done.13, ...), custom_call_target="tpu_custom_call" | custom-call | flops 4292000000 | bytes 13616000 | tf_op jit(solution)/shard_map/attend_back/pallas_call | solution.py:986
  376.6 3.4 collective-permute-done.33.got_p
  382.5 2.6 fold_plane.6
  385.1 5.4 %input_back.2.refs_3_ = bf16[1024,1024]{1,0:T(8,128)(2,1)} custom-call(bf16[2048,768]{1,0:T(8,128)(2,1)S(1)} %bitcast.150, bf16[2048,768]{1,0:T(8,128)(2,1)S(1)} %bitcast.153, bf16[1024,1536]{1,0:T(8,128)(2,1)S(1)} %copy-done.1, bf16[1024,1536]{1,0:T(8,128)(2,1)S(1)} %copy-done.1, bf16[4,32,1280]{2,1,0:T(8,128)(2,1)} %get-tuple-element.165.rest_0_, ...), custom_call_target="tpu_custom_call" | custom-call | flops 1450000000 | bytes 4600000 | tf_op jit(solution)/shard_map/input_back/pallas_call | solution.py:363
  397.2 5.5 %product.15 = bf16[1024,768]{1,0:T(8,128)(2,1)S(1)} custom-call(s32[4]{0:T(128)S(1)} %pad_add_fusion.1.where_ref, bf16[1024,1024]{1,0:T(8,128)(2,1)S(1)} %bitcast.172, bf16[1024,1024]{1,0:T(8,128)(2,1)} %collective-permute-done.theirs_ref.refs_1_, bf16[2048,768]{1,0:T(8,128)(2,1)S(1)} %bitcast.154, bf16[1024,1024]{1,0:T(8,128)(2,1)} %input_back.2.refs_3_), custom_call_target="tpu_custom_call" | custom-call | flops 1224155392 | bytes 3883527 | tf_op jit(solution)/shard_map/product/pallas_call | solution.py:806
  402.7 3.8 collective-permute-done.39.got_p
  411.6 3.5 collective-permute-done.38.refs_6_
  415.6 6.2 %update.3 = (f32[512,1024]{1,0:T(8,128)}, f32[512,1024]{1,0:T(8,128)}, f32[512,1024]{1,0:T(8,128)}, bf16[512,1024]{1,0:T(8,128)(2,1)}) custom-call(s32[4]{0:T(128)S(1)} %pad_add_fusion.1.where_ref, f32[512,1024]{1,0:T(8,128)S(1)} %copy-done.24, f32[512,1024]{1,0:T(8,128)S(1)} %copy-done.28, f32[512,1024]{1,0:T(8,128)S(1)} %copy-done.29, ...), custom_call_target="tpu_custom_call" | custom-call | flops 1450000000 | bytes 4600000 | tf_op jit(solution)/shard_map/update/pallas_call | solution.py:331
  423.4 6.8 %input_back.3.rest_0_ = f32[1024,1024]{1,0:T(8,128)} custom-call(bf16[2048,768]{1,0:T(8,128)(2,1)S(1)} %bitcast.151, bf16[2048,768]{1,0:T(8,128)(2,1)S(1)} %bitcast.155, bf16[1024,1536]{1,0:T(8,128)(2,1)S(1)} %copy-done.1, bf16[1024,1536]{1,0:T(8,128)(2,1)S(1)} %copy-done.1, bf16[1024,1024]{1,0:T(8,128)(2,1)S(1)} %copy-done.11, ...), custom_call_target="tpu_custom_call" | custom-call | flops 1450000000 | bytes 4600000 | tf_op jit(solution)/shard_map/input_back/pallas_call | solution.py:363
  430.2 2.2 copy-done.14
  434.1 2.7 collective-permute-start.46
  439.5 4.3 collective-permute-done.47.got_p
  444.9 3.7 collective-permute-done.46.rest_1_
  452.1 3.4 collective-permute-start.45
  455.5 7.0 %collective-permute-done.52.got = bf16[2,2,32,896]{3,2,1,0:T(8,128)(2,1)S(1)} collective-permute-done((bf16[2,2,32,896]{3,2,1,0:T(8,128)(2,1)S(1)}, bf16[2,2,32,896]{3,2,1,0:T(8,128)(2,1)S(1)}, u32[]{:S(2)}, u32[]{:S(2)}) %collective-permute-start.52) | collective-permute-done | bytes 229408 | tf_op jit(solution)/shard_map/ppermute | solution.py:139
  464.8 5.1 %update.4 = (f32[128,4096]{1,0:T(8,128)}, f32[128,4096]{1,0:T(8,128)}, f32[128,4096]{1,0:T(8,128)}, bf16[128,4096]{1,0:T(8,128)(2,1)}) custom-call(s32[4]{0:T(128)S(1)} %pad_add_fusion.1.where_ref, f32[128,4096]{1,0:T(8,128)S(1)} %copy-done.25, f32[128,4096]{1,0:T(8,128)S(1)} %copy-done.30, f32[128,4096]{1,0:T(8,128)S(1)} %copy-done.31, ...), custom_call_target="tpu_custom_call" | custom-call | flops 1450000000 | bytes 4600000 | tf_op jit(solution)/shard_map/update/pallas_call | solution.py:331
  475.8 2.4 collective-permute-done.57.refs_8_
  478.2 5.9 %collective-permute-done.59.refs_10_ = bf16[2,32,896]{2,1,0:T(8,128)(2,1)S(1)} collective-permute-done((bf16[2,32,896]{2,1,0:T(8,128)(2,1)S(1)}, bf16[2,32,896]{2,1,0:T(8,128)(2,1)S(1)}, u32[]{:S(2)}, u32[]{:S(2)}) %collective-permute-start.59) | collective-permute-done | bytes 114720 | tf_op jit(solution)/shard_map/ppermute | solution.py:143
  488.0 5.4 %update.5 = (f32[4,128,1024]{2,1,0:T(8,128)}, f32[4,128,1024]{2,1,0:T(8,128)}, f32[4,128,1024]{2,1,0:T(8,128)}, bf16[4,128,1024]{2,1,0:T(8,128)(2,1)}) custom-call(s32[4]{0:T(128)S(1)} %pad_add_fusion.1.where_ref, f32[4,128,1024]{2,1,0:T(8,128)S(1)} %copy-done.21, f32[4,128,1024]{2,1,0:T(8,128)S(1)} %copy-done.32, f32[4,128,1024]{2,1,0:T(8,128)S(1)} %copy-done.33, ...), custom_call_target="tpu_custom_call" | custom-call | flops 1450000000 | bytes 4600000 | tf_op jit(solution)/shard_map/update/pallas_call | solution.py:331
  (336 shorter events, 112.3 us)
Async XLA Ops:
  2.8 11.0 %collective-permute-start.1 = (bf16[144,768]{1,0:T(8,128)(2,1)S(1)}, bf16[144,768]{1,0:T(8,128)(2,1)S(1)}, u32[]{:S(2)}, u32[]{:S(2)}) collective-permute-start(bf16[144,768]{1,0:T(8,128)(2,1)S(1)} %get-tuple-element.212), channel_id=1, source_target_pairs={{0,12},{2,14},{4,0},{6,2},{8,4},{10,6},{12,8},{14,10},{1,13},{3,15... | collective-permute-start | bytes 663560 | tf_op jit(solution)/shard_map/ppermute | solution.py:77
  7.9 18.9 %collective-permute-start.2 = (bf16[144,768]{1,0:T(8,128)(2,1)S(1)}, bf16[144,768]{1,0:T(8,128)(2,1)}, u32[]{:S(2)}, u32[]{:S(2)}) collective-permute-start(bf16[144,768]{1,0:T(8,128)(2,1)S(1)} %get-tuple-element.212), channel_id=1, source_target_pairs={{0,8},{2,10},{4,12},{6,14},{8,0},{10,2},{12,4},{14,6},{1,9},{3,11}... | collective-permute-start | bytes 663560 | tf_op jit(solution)/shard_map/ppermute | solution.py:77
  7.9 18.9 %collective-permute-start.3 = (bf16[144,768]{1,0:T(8,128)(2,1)S(1)}, bf16[144,768]{1,0:T(8,128)(2,1)S(1)}, u32[]{:S(2)}, u32[]{:S(2)}) collective-permute-start(bf16[144,768]{1,0:T(8,128)(2,1)S(1)} %get-tuple-element.212), channel_id=1, source_target_pairs={{0,4},{2,6},{4,8},{6,10},{8,12},{10,14},{12,0},{14,2},{1,5},{3,7},... | collective-permute-start | bytes 663560 | tf_op jit(solution)/shard_map/ppermute | solution.py:77
  8.9 60.9 %collective-permute-start = (bf16[1024,1024]{1,0:T(8,128)(2,1)S(1)}, bf16[1024,1024]{1,0:T(8,128)(2,1)}, u32[]{:S(2)}, u32[]{:S(2)}) collective-permute-start(bf16[1024,1024]{1,0:T(8,128)(2,1)S(1)} %bitcast.169), channel_id=1, source_target_pairs={{0,1},{1,0},{2,3},{3,2},{4,5},{5,4},{6,7},{7,6},{8,9},{9,8},{10,11... | collective-permute-start | bytes 6291464 | tf_op jit(solution)/shard_map/ppermute | solution.py:69
  28.6 20.7 %collective-permute-start.4 = (bf16[4,144,768]{2,1,0:T(8,128)(2,1)S(1)}, bf16[4,144,768]{2,1,0:T(8,128)(2,1)}, u32[]{:S(2)}, u32[]{:S(2)}) collective-permute-start(bf16[4,144,768]{2,1,0:T(8,128)(2,1)S(1)} %pad_maximum_fusion.rest_1_.rest_0_), channel_id=1, source_target_pairs={{0,2},{2,0},{4,6},{6,4},{8,10},{10,8},{12,14},{14,12},{1,3},{3,1},... | collective-permute-start | bytes 2654216 | tf_op jit(solution)/shard_map/ppermute | solution.py:85
  30.2 20.3 %collective-permute-start.5 = (bf16[4,144,768]{2,1,0:T(8,128)(2,1)S(1)}, bf16[4,144,768]{2,1,0:T(8,128)(2,1)}, u32[]{:S(2)}, u32[]{:S(2)}) collective-permute-start(bf16[4,144,768]{2,1,0:T(8,128)(2,1)S(1)} %pad_maximum_fusion.rest_1_.rest_0_), channel_id=1, source_target_pairs={{0,16},{16,0},{1,17},{17,1},{2,18},{18,2},{3,19},{19,3},{4,20},{20... | collective-permute-start | bytes 2654216 | tf_op jit(solution)/shard_map/ppermute | solution.py:90
  34.9 29.0 %collective-permute-start.8 = (bf16[304,1024]{1,0:T(8,128)(2,1)S(1)}, bf16[304,1024]{1,0:T(8,128)(2,1)S(1)}, u32[]{:S(2)}, u32[]{:S(2)}) collective-permute-start(bf16[304,1024]{1,0:T(8,128)(2,1)S(1)} %relay.2.own), channel_id=1, source_target_pairs={{0,8},{2,10},{4,12},{6,14},{8,0},{10,2},{12,4},{14,6},{1,9},{3,11}... | collective-permute-start | bytes 1867784 | tf_op jit(solution)/shard_map/ppermute | solution.py:139
  52.1 11.8 %collective-permute-start.6 = (bf16[2,144,768]{2,1,0:T(8,128)(2,1)S(1)}, bf16[2,144,768]{2,1,0:T(8,128)(2,1)S(1)}, u32[]{:S(2)}, u32[]{:S(2)}) collective-permute-start(bf16[2,144,768]{2,1,0:T(8,128)(2,1)S(1)} %get-tuple-element.111), channel_id=1, source_target_pairs={{0,2},{2,0},{4,6},{6,4},{8,10},{10,8},{12,14},{14,12},{1,3},{3,1},... | collective-permute-start | bytes 1327112 | tf_op jit(solution)/shard_map/ppermute | solution.py:85
  52.7 11.2 %collective-permute-start.7 = (bf16[2,144,768]{2,1,0:T(8,128)(2,1)S(1)}, bf16[2,144,768]{2,1,0:T(8,128)(2,1)S(1)}, u32[]{:S(2)}, u32[]{:S(2)}) collective-permute-start(bf16[2,144,768]{2,1,0:T(8,128)(2,1)S(1)} %get-tuple-element.112), channel_id=1, source_target_pairs={{0,16},{16,0},{1,17},{17,1},{2,18},{18,2},{3,19},{19,3},{4,20},{20... | collective-permute-start | bytes 1327112 | tf_op jit(solution)/shard_map/ppermute | solution.py:90
  65.5 29.5 %collective-permute-start.9 = (bf16[2,304,1024]{2,1,0:T(8,128)(2,1)}, bf16[2,304,1024]{2,1,0:T(8,128)(2,1)}, u32[]{:S(2)}, u32[]{:S(2)}) collective-permute-start(bf16[2,304,1024]{2,1,0:T(8,128)(2,1)} %pair.1.rest_5_.rest_0_), channel_id=1, source_target_pairs={{0,4},{2,6},{4,0},{6,2},{8,12},{10,14},{12,8},{14,10},{1,5},{3,7},... | collective-permute-start | bytes 3735560 | tf_op jit(solution)/shard_map/ppermute | solution.py:139
  67.0 50.7 %collective-permute-start.11 = (bf16[2,304,1024]{2,1,0:T(8,128)(2,1)}, bf16[2,304,1024]{2,1,0:T(8,128)(2,1)}, u32[]{:S(2)}, u32[]{:S(2)}) collective-permute-start(bf16[2,304,1024]{2,1,0:T(8,128)(2,1)} %pair.1.rest_5_.rest_0_), channel_id=1, source_target_pairs={{0,2},{2,0},{4,6},{6,4},{8,10},{10,8},{12,14},{14,12},{1,3},{3,1},... | collective-permute-start | bytes 3735560 | tf_op jit(solution)/shard_map/ppermute | solution.py:85
  68.3 49.5 %collective-permute-start.13 = (bf16[2,304,1024]{2,1,0:T(8,128)(2,1)}, bf16[2,304,1024]{2,1,0:T(8,128)(2,1)}, u32[]{:S(2)}, u32[]{:S(2)}) collective-permute-start(bf16[2,304,1024]{2,1,0:T(8,128)(2,1)} %pair.1.rest_5_.rest_0_), channel_id=1, source_target_pairs={{0,16},{16,0},{1,17},{17,1},{2,18},{18,2},{3,19},{19,3},{4,20},{20... | collective-permute-start | bytes 3735560 | tf_op jit(solution)/shard_map/ppermute | solution.py:90
  98.3 28.3 %collective-permute-start.12 = (bf16[2,304,1024]{2,1,0:T(8,128)(2,1)S(1)}, bf16[2,304,1024]{2,1,0:T(8,128)(2,1)S(1)}, u32[]{:S(2)}, u32[]{:S(2)}) collective-permute-start(bf16[2,304,1024]{2,1,0:T(8,128)(2,1)S(1)} %relay.3.rest_0_.rest_1_), channel_id=1, source_target_pairs={{0,2},{2,0},{4,6},{6,4},{8,10},{10,8},{12,14},{14,12},{1,3},{3,1},... | collective-permute-start | bytes 3735560 | tf_op jit(solution)/shard_map/ppermute | solution.py:85
  98.9 28.1 %collective-permute-start.14 = (bf16[2,304,1024]{2,1,0:T(8,128)(2,1)S(1)}, bf16[2,304,1024]{2,1,0:T(8,128)(2,1)}, u32[]{:S(2)}, u32[]{:S(2)}) collective-permute-start(bf16[2,304,1024]{2,1,0:T(8,128)(2,1)S(1)} %relay.3.rest_0_.rest_1_), channel_id=1, source_target_pairs={{0,16},{16,0},{1,17},{17,1},{2,18},{18,2},{3,19},{19,3},{4,20},{20... | collective-permute-start | bytes 3735560 | tf_op jit(solution)/shard_map/ppermute | solution.py:90
  133.1 38.2 %collective-permute-start.17 = (bf16[12,304,1024]{2,1,0:T(8,128)(2,1)}, bf16[12,304,1024]{2,1,0:T(8,128)(2,1)}, u32[]{:S(2)}, u32[]{:S(2)}) collective-permute-start(bf16[12,304,1024]{2,1,0:T(8,128)(2,1)} %get-tuple-element.120.more_0_), channel_id=1, source_target_pairs={{0,1},{1,0},{2,3},{3,2},{4,5},{5,4},{6,7},{7,6},{8,9},{9,8},{10,11... | collective-permute-start | bytes 22413320 | tf_op jit(solution)/shard_map/ppermute | solution.py:69
  133.1 29.8 %collective-permute-start.15 = (bf16[2,304,1024]{2,1,0:T(8,128)(2,1)S(1)}, bf16[2,304,1024]{2,1,0:T(8,128)(2,1)S(1)}, u32[]{:S(2)}, u32[]{:S(2)}) collective-permute-start(bf16[2,304,1024]{2,1,0:T(8,128)(2,1)S(1)} %get-tuple-element.121), channel_id=1, source_target_pairs={{0,2},{2,0},{4,6},{6,4},{8,10},{10,8},{12,14},{14,12},{1,3},{3,1},... | collective-permute-start | bytes 3735560 | tf_op jit(solution)/shard_map/ppermute | solution.py:85
  134.6 29.5 %collective-permute-start.16 = (bf16[2,304,1024]{2,1,0:T(8,128)(2,1)S(1)}, bf16[2,304,1024]{2,1,0:T(8,128)(2,1)S(1)}, u32[]{:S(2)}, u32[]{:S(2)}) collective-permute-start(bf16[2,304,1024]{2,1,0:T(8,128)(2,1)S(1)} %get-tuple-element.122), channel_id=1, source_target_pairs={{0,16},{16,0},{1,17},{17,1},{2,18},{18,2},{3,19},{19,3},{4,20},{20... | collective-permute-start | bytes 3735560 | tf_op jit(solution)/shard_map/ppermute | solution.py:90
  244.8 34.1 %collective-permute-start.21 = (bf16[4,2,128,512]{3,2,1,0:T(8,128)(2,1)S(1)}, bf16[4,2,128,512]{3,2,1,0:T(8,128)(2,1)S(1)}, u32[]{:S(2)}, u32[]{:S(2)}) collective-permute-start(bf16[4,2,128,512]{3,2,1,0:T(8,128)(2,1)S(1)} %get-tuple-element.132.after_ref), channel_id=1, source_target_pairs={{0,2},{2,0},{4,6},{6,4},{8,10},{10,8},{12,14},{14,12},{1,3},{3,1},... | collective-permute-start | bytes 3145736 | tf_op jit(solution)/shard_map/ppermute | solution.py:85
  245.4 33.5 %collective-permute-start.22 = (bf16[4,2,128,512]{3,2,1,0:T(8,128)(2,1)S(1)}, bf16[4,2,128,512]{3,2,1,0:T(8,128)(2,1)S(1)}, u32[]{:S(2)}, u32[]{:S(2)}) collective-permute-start(bf16[4,2,128,512]{3,2,1,0:T(8,128)(2,1)S(1)} %get-tuple-element.138), channel_id=1, source_target_pairs={{0,16},{16,0},{1,17},{17,1},{2,18},{18,2},{3,19},{19,3},{4,20},{20... | collective-permute-start | bytes 3145736 | tf_op jit(solution)/shard_map/ppermute | solution.py:90
  284.0 13.5 %collective-permute-start.23 = (bf16[4,128,512]{2,1,0:T(8,128)(2,1)S(1)}, bf16[4,128,512]{2,1,0:T(8,128)(2,1)S(1)}, u32[]{:S(2)}, u32[]{:S(2)}) collective-permute-start(bf16[4,128,512]{2,1,0:T(8,128)(2,1)S(1)} %get-tuple-element.141.refs_2_), channel_id=1, source_target_pairs={{0,16},{16,0},{1,17},{17,1},{2,18},{18,2},{3,19},{19,3},{4,20},{20... | collective-permute-start | bytes 1572872 | tf_op jit(solution)/shard_map/ppermute | solution.py:90
  285.8 13.1 %collective-permute-start.24 = (bf16[4,128,512]{2,1,0:T(8,128)(2,1)S(1)}, bf16[4,128,512]{2,1,0:T(8,128)(2,1)S(1)}, u32[]{:S(2)}, u32[]{:S(2)}) collective-permute-start(bf16[4,128,512]{2,1,0:T(8,128)(2,1)S(1)} %get-tuple-element.143.refs_3_), channel_id=1, source_target_pairs={{0,2},{2,0},{4,6},{6,4},{8,10},{10,8},{12,14},{14,12},{1,3},{3,1},... | collective-permute-start | bytes 1572872 | tf_op jit(solution)/shard_map/ppermute | solution.py:85
  307.0 15.1 %collective-permute-start.20 = (bf16[1024,512]{1,0:T(8,128)(2,1)S(1)}, bf16[1024,512]{1,0:T(8,128)(2,1)S(1)}, u32[]{:S(2)}, u32[]{:S(2)}) collective-permute-start(bf16[1024,512]{1,0:T(8,128)(2,1)S(1)} %get-tuple-element.134), channel_id=1, source_target_pairs={{0,1},{1,0},{2,3},{3,2},{4,5},{5,4},{6,7},{7,6},{8,9},{9,8},{10,11... | collective-permute-start | bytes 3145736 | tf_op jit(solution)/shard_map/ppermute | solution.py:69
  307.5 13.8 %collective-permute-start.25 = (bf16[2,2,128,512]{3,2,1,0:T(8,128)(2,1)S(1)}, bf16[2,2,128,512]{3,2,1,0:T(8,128)(2,1)S(1)}, u32[]{:S(2)}, u32[]{:S(2)}) collective-permute-start(bf16[2,2,128,512]{3,2,1,0:T(8,128)(2,1)S(1)} %get-tuple-element.146.refs_2_), channel_id=1, source_target_pairs={{0,4},{2,6},{4,0},{6,2},{8,12},{10,14},{12,8},{14,10},{1,5},{3,7},... | collective-permute-start | bytes 1572872 | tf_op jit(solution)/shard_map/ppermute | solution.py:139
  317.9 27.6 %collective-permute-start.29 = (bf16[4,2,32,2048]{3,2,1,0:T(8,128)(2,1)S(1)}, bf16[4,2,32,2048]{3,2,1,0:T(8,128)(2,1)S(1)}, u32[]{:S(2)}, u32[]{:S(2)}) collective-permute-start(bf16[4,2,32,2048]{3,2,1,0:T(8,128)(2,1)S(1)} %get-tuple-element.148.rest_0_), channel_id=1, source_target_pairs={{0,2},{2,0},{4,6},{6,4},{8,10},{10,8},{12,14},{14,12},{1,3},{3,1},... | collective-permute-start | bytes 3145736 | tf_op jit(solution)/shard_map/ppermute | solution.py:85
  319.5 26.0 %collective-permute-start.30 = (bf16[4,2,32,2048]{3,2,1,0:T(8,128)(2,1)S(1)}, bf16[4,2,32,2048]{3,2,1,0:T(8,128)(2,1)S(1)}, u32[]{:S(2)}, u32[]{:S(2)}) collective-permute-start(bf16[4,2,32,2048]{3,2,1,0:T(8,128)(2,1)S(1)} %get-tuple-element.149.rest_1_), channel_id=1, source_target_pairs={{0,16},{16,0},{1,17},{17,1},{2,18},{18,2},{3,19},{19,3},{4,20},{20... | collective-permute-start | bytes 3145736 | tf_op jit(solution)/shard_map/ppermute | solution.py:90
  320.0 27.4 %collective-permute-start.28 = (bf16[1024,512]{1,0:T(8,128)(2,1)S(1)}, bf16[1024,512]{1,0:T(8,128)(2,1)S(1)}, u32[]{:S(2)}, u32[]{:S(2)}) collective-permute-start(bf16[1024,512]{1,0:T(8,128)(2,1)S(1)} %product.12.refs_3_), channel_id=1, source_target_pairs={{0,1},{1,0},{2,3},{3,2},{4,5},{5,4},{6,7},{7,6},{8,9},{9,8},{10,11... | collective-permute-start | bytes 3145736 | tf_op jit(solution)/shard_map/ppermute | solution.py:69
  322.0 15.3 %collective-permute-start.27 = (bf16[2,128,512]{2,1,0:T(8,128)(2,1)S(1)}, bf16[2,128,512]{2,1,0:T(8,128)(2,1)S(1)}, u32[]{:S(2)}, u32[]{:S(2)}) collective-permute-start(bf16[2,128,512]{2,1,0:T(8,128)(2,1)S(1)} %get-tuple-element.150.refs_8_), channel_id=1, source_target_pairs={{0,8},{2,10},{4,12},{6,14},{8,0},{10,2},{12,4},{14,6},{1,9},{3,11}... | collective-permute-start | bytes 786440 | tf_op jit(solution)/shard_map/ppermute | solution.py:139
  351.5 31.0 %collective-permute-start.31 = (bf16[4,2,32,1280]{3,2,1,0:T(8,128)(2,1)}, bf16[4,2,32,1280]{3,2,1,0:T(8,128)(2,1)}, u32[]{:S(2)}, u32[]{:S(2)}) collective-permute-start(bf16[4,2,32,1280]{3,2,1,0:T(8,128)(2,1)} %get-tuple-element.157.refs_8_), channel_id=1, source_target_pairs={{0,2},{2,0},{4,6},{6,4},{8,10},{10,8},{12,14},{14,12},{1,3},{3,1},... | collective-permute-start | bytes 1966088 | tf_op jit(solution)/shard_map/ppermute | solution.py:85
  353.0 29.5 %collective-permute-start.32 = (bf16[4,2,32,1280]{3,2,1,0:T(8,128)(2,1)}, bf16[4,2,32,1280]{3,2,1,0:T(8,128)(2,1)}, u32[]{:S(2)}, u32[]{:S(2)}) collective-permute-start(bf16[4,2,32,1280]{3,2,1,0:T(8,128)(2,1)} %get-tuple-element.158.refs_9_), channel_id=1, source_target_pairs={{0,16},{16,0},{1,17},{17,1},{2,18},{18,2},{3,19},{19,3},{4,20},{20... | collective-permute-start | bytes 1966088 | tf_op jit(solution)/shard_map/ppermute | solution.py:90
  353.5 26.6 %collective-permute-start.33 = (bf16[4,32,2048]{2,1,0:T(8,128)(2,1)S(1)}, bf16[4,32,2048]{2,1,0:T(8,128)(2,1)}, u32[]{:S(2)}, u32[]{:S(2)}) collective-permute-start(bf16[4,32,2048]{2,1,0:T(8,128)(2,1)S(1)} %get-tuple-element.155.refs_12_), channel_id=1, source_target_pairs={{0,16},{16,0},{1,17},{17,1},{2,18},{18,2},{3,19},{19,3},{4,20},{20... | collective-permute-start | bytes 1572872 | tf_op jit(solution)/shard_map/ppermute | solution.py:90
  355.0 25.0 %collective-permute-start.34 = (bf16[4,32,2048]{2,1,0:T(8,128)(2,1)S(1)}, bf16[4,32,2048]{2,1,0:T(8,128)(2,1)}, u32[]{:S(2)}, u32[]{:S(2)}) collective-permute-start(bf16[4,32,2048]{2,1,0:T(8,128)(2,1)S(1)} %get-tuple-element.156.refs_13_), channel_id=1, source_target_pairs={{0,2},{2,0},{4,6},{6,4},{8,10},{10,8},{12,14},{14,12},{1,3},{3,1},... | collective-permute-start | bytes 1572872 | tf_op jit(solution)/shard_map/ppermute | solution.py:85
  390.5 31.3 %collective-permute-start.35 = (bf16[1024,1024]{1,0:T(8,128)(2,1)}, bf16[1024,1024]{1,0:T(8,128)(2,1)}, u32[]{:S(2)}, u32[]{:S(2)}) collective-permute-start(bf16[1024,1024]{1,0:T(8,128)(2,1)} %input_back.2.refs_3_), channel_id=1, source_target_pairs={{0,1},{1,0},{2,3},{3,2},{4,5},{5,4},{6,7},{7,6},{8,9},{9,8},{10,11... | collective-permute-start | bytes 6291464 | tf_op jit(solution)/shard_map/ppermute | solution.py:69
  390.6 18.9 %collective-permute-start.36 = (bf16[2,128,512]{2,1,0:T(8,128)(2,1)S(1)}, bf16[2,128,512]{2,1,0:T(8,128)(2,1)}, u32[]{:S(2)}, u32[]{:S(2)}) collective-permute-start(bf16[2,128,512]{2,1,0:T(8,128)(2,1)S(1)} %fold_line.4.refs_3_), channel_id=1, source_target_pairs={{0,16},{16,0},{1,17},{17,1},{2,18},{18,2},{3,19},{19,3},{4,20},{20... | collective-permute-start | bytes 786440 | tf_op jit(solution)/shard_map/ppermute | solution.py:90
  391.2 19.6 %collective-permute-start.37 = (bf16[2,128,512]{2,1,0:T(8,128)(2,1)S(1)}, bf16[2,128,512]{2,1,0:T(8,128)(2,1)}, u32[]{:S(2)}, u32[]{:S(2)}) collective-permute-start(bf16[2,128,512]{2,1,0:T(8,128)(2,1)S(1)} %fold_line.4.refs_3_), channel_id=1, source_target_pairs={{0,1},{1,0},{2,3},{3,2},{4,5},{5,4},{6,7},{7,6},{8,9},{9,8},{10,11... | collective-permute-start | bytes 786440 | tf_op jit(solution)/shard_map/ppermute | solution.py:69
  391.5 15.0 %collective-permute-start.39 = (bf16[4,32,1280]{2,1,0:T(8,128)(2,1)}, bf16[4,32,1280]{2,1,0:T(8,128)(2,1)}, u32[]{:S(2)}, u32[]{:S(2)}) collective-permute-start(bf16[4,32,1280]{2,1,0:T(8,128)(2,1)} %get-tuple-element.165.rest_0_), channel_id=1, source_target_pairs={{0,16},{16,0},{1,17},{17,1},{2,18},{18,2},{3,19},{19,3},{4,20},{20... | collective-permute-start | bytes 983048 | tf_op jit(solution)/shard_map/ppermute | solution.py:90
  393.0 13.5 %collective-permute-start.40 = (bf16[4,32,1280]{2,1,0:T(8,128)(2,1)}, bf16[4,32,1280]{2,1,0:T(8,128)(2,1)}, u32[]{:S(2)}, u32[]{:S(2)}) collective-permute-start(bf16[4,32,1280]{2,1,0:T(8,128)(2,1)} %get-tuple-element.166.rest_1_), channel_id=1, source_target_pairs={{0,2},{2,0},{4,6},{6,4},{8,10},{10,8},{12,14},{14,12},{1,3},{3,1},... | collective-permute-start | bytes 983048 | tf_op jit(solution)/shard_map/ppermute | solution.py:85
  406.5 26.6 %collective-permute-start.42 = (bf16[2,2,32,2048]{3,2,1,0:T(8,128)(2,1)S(1)}, bf16[2,2,32,2048]{3,2,1,0:T(8,128)(2,1)S(1)}, u32[]{:S(2)}, u32[]{:S(2)}) collective-permute-start(bf16[2,2,32,2048]{3,2,1,0:T(8,128)(2,1)S(1)} %copy-done.44), channel_id=1, source_target_pairs={{0,4},{2,6},{4,0},{6,2},{8,12},{10,14},{12,8},{14,10},{1,5},{3,7},... | collective-permute-start | bytes 1572872 | tf_op jit(solution)/shard_map/ppermute | solution.py:139
  409.5 20.7 %collective-permute-start.43 = (bf16[4,2,32,896]{3,2,1,0:T(8,128)(2,1)S(1)}, bf16[4,2,32,896]{3,2,1,0:T(8,128)(2,1)S(1)}, u32[]{:S(2)}, u32[]{:S(2)}) collective-permute-start(bf16[4,2,32,896]{3,2,1,0:T(8,128)(2,1)S(1)} %get-tuple-element.174.refs_7_), channel_id=1, source_target_pairs={{0,2},{2,0},{4,6},{6,4},{8,10},{10,8},{12,14},{14,12},{1,3},{3,1},... | collective-permute-start | bytes 1376264 | tf_op jit(solution)/shard_map/ppermute | solution.py:85
  410.9 19.3 %collective-permute-start.44 = (bf16[4,2,32,896]{3,2,1,0:T(8,128)(2,1)S(1)}, bf16[4,2,32,896]{3,2,1,0:T(8,128)(2,1)S(1)}, u32[]{:S(2)}, u32[]{:S(2)}) collective-permute-start(bf16[4,2,32,896]{3,2,1,0:T(8,128)(2,1)S(1)} %get-tuple-element.175.refs_8_), channel_id=1, source_target_pairs={{0,16},{16,0},{1,17},{17,1},{2,18},{18,2},{3,19},{19,3},{4,20},{20... | collective-permute-start | bytes 1376264 | tf_op jit(solution)/shard_map/ppermute | solution.py:90
  415.1 23.7 %collective-permute-start.41 = (bf16[2,2,32,1280]{3,2,1,0:T(8,128)(2,1)S(1)}, bf16[2,2,32,1280]{3,2,1,0:T(8,128)(2,1)S(1)}, u32[]{:S(2)}, u32[]{:S(2)}) collective-permute-start(bf16[2,2,32,1280]{3,2,1,0:T(8,128)(2,1)S(1)} %get-tuple-element.173.refs_8_), channel_id=1, source_target_pairs={{0,4},{2,6},{4,0},{6,2},{8,12},{10,14},{12,8},{14,10},{1,5},{3,7},... | collective-permute-start | bytes 983048 | tf_op jit(solution)/shard_map/ppermute | solution.py:139
  434.1 14.5 %collective-permute-start.46 = (bf16[2,32,2048]{2,1,0:T(8,128)(2,1)S(1)}, bf16[2,32,2048]{2,1,0:T(8,128)(2,1)S(1)}, u32[]{:S(2)}, u32[]{:S(2)}) collective-permute-start(bf16[2,32,2048]{2,1,0:T(8,128)(2,1)S(1)} %get-tuple-element.183.rest_0_), channel_id=1, source_target_pairs={{0,8},{2,10},{4,12},{6,14},{8,0},{10,2},{12,4},{14,6},{1,9},{3,11}... | collective-permute-start | bytes 786440 | tf_op jit(solution)/shard_map/ppermute | solution.py:139
  449.2 15.5 %collective-permute-start.49 = (bf16[2,32,2048]{2,1,0:T(8,128)(2,1)S(1)}, bf16[2,32,2048]{2,1,0:T(8,128)(2,1)S(1)}, u32[]{:S(2)}, u32[]{:S(2)}) collective-permute-start(bf16[2,32,2048]{2,1,0:T(8,128)(2,1)S(1)} %fold_line.5.rest_0_.refs_3_), channel_id=1, source_target_pairs={{0,16},{16,0},{1,17},{17,1},{2,18},{18,2},{3,19},{19,3},{4,20},{20... | collective-permute-start | bytes 786440 | tf_op jit(solution)/shard_map/ppermute | solution.py:90
  450.1 14.6 %collective-permute-start.50 = (bf16[2,32,2048]{2,1,0:T(8,128)(2,1)S(1)}, bf16[2,32,2048]{2,1,0:T(8,128)(2,1)S(1)}, u32[]{:S(2)}, u32[]{:S(2)}) collective-permute-start(bf16[2,32,2048]{2,1,0:T(8,128)(2,1)S(1)} %fold_line.5.rest_0_.refs_3_), channel_id=1, source_target_pairs={{0,1},{1,0},{2,3},{3,2},{4,5},{5,4},{6,7},{7,6},{8,9},{9,8},{10,11... | collective-permute-start | bytes 786440 | tf_op jit(solution)/shard_map/ppermute | solution.py:69
  450.1 14.6 %collective-permute-start.51 = (bf16[2,32,2048]{2,1,0:T(8,128)(2,1)S(1)}, bf16[2,32,2048]{2,1,0:T(8,128)(2,1)S(1)}, u32[]{:S(2)}, u32[]{:S(2)}) collective-permute-start(bf16[2,32,2048]{2,1,0:T(8,128)(2,1)S(1)} %fold_line.5.rest_0_.refs_3_), channel_id=1, source_target_pairs={{0,17},{1,16},{16,1},{17,0},{2,19},{3,18},{18,3},{19,2},{4,21},{5,... | collective-permute-start | bytes 786440 | tf_op jit(solution)/shard_map/ppermute | solution.py:143
  451.4 11.0 %collective-permute-start.52 = (bf16[2,2,32,896]{3,2,1,0:T(8,128)(2,1)S(1)}, bf16[2,2,32,896]{3,2,1,0:T(8,128)(2,1)S(1)}, u32[]{:S(2)}, u32[]{:S(2)}) collective-permute-start(bf16[2,2,32,896]{3,2,1,0:T(8,128)(2,1)S(1)} %get-tuple-element.189.rest_2_), channel_id=1, source_target_pairs={{0,4},{2,6},{4,0},{6,2},{8,12},{10,14},{12,8},{14,10},{1,5},{3,7},... | collective-permute-start | bytes 688136 | tf_op jit(solution)/shard_map/ppermute | solution.py:139
  452.1 17.8 %collective-permute-start.45 = (bf16[2,32,1280]{2,1,0:T(8,128)(2,1)S(1)}, bf16[2,32,1280]{2,1,0:T(8,128)(2,1)S(1)}, u32[]{:S(2)}, u32[]{:S(2)}) collective-permute-start(bf16[2,32,1280]{2,1,0:T(8,128)(2,1)S(1)} %get-tuple-element.185.rest_0_), channel_id=1, source_target_pairs={{0,8},{2,10},{4,12},{6,14},{8,0},{10,2},{12,4},{14,6},{1,9},{3,11}... | collective-permute-start | bytes 491528 | tf_op jit(solution)/shard_map/ppermute | solution.py:139
  473.7 11.1 %collective-permute-start.53 = (bf16[2,32,1280]{2,1,0:T(8,128)(2,1)S(1)}, bf16[2,32,1280]{2,1,0:T(8,128)(2,1)S(1)}, u32[]{:S(2)}, u32[]{:S(2)}) collective-permute-start(bf16[2,32,1280]{2,1,0:T(8,128)(2,1)S(1)} %fold_line.6.rest_2_.refs_3_), channel_id=1, source_target_pairs={{0,16},{16,0},{1,17},{17,1},{2,18},{18,2},{3,19},{19,3},{4,20},{20... | collective-permute-start | bytes 491528 | tf_op jit(solution)/shard_map/ppermute | solution.py:90
  474.9 9.9 %collective-permute-start.55 = (bf16[2,32,1280]{2,1,0:T(8,128)(2,1)S(1)}, bf16[2,32,1280]{2,1,0:T(8,128)(2,1)S(1)}, u32[]{:S(2)}, u32[]{:S(2)}) collective-permute-start(bf16[2,32,1280]{2,1,0:T(8,128)(2,1)S(1)} %fold_line.6.rest_2_.refs_3_), channel_id=1, source_target_pairs={{0,17},{1,16},{16,1},{17,0},{2,19},{3,18},{18,3},{19,2},{4,21},{5,... | collective-permute-start | bytes 491528 | tf_op jit(solution)/shard_map/ppermute | solution.py:143
  (89 other events, 659.0 us)
